TPU v7x, 32 devices: a whole 2x2x4 slice. The times are simulated.
32 devices in a mesh: group: 2 (over y), ep: 16 (over z, x, core).
Axes of the slice: x: 2, y: 2, z: 4, core: 2. Of those that a mesh axis runs over, the one named last changes fastest.
Arguments:
- queries: bfloat16 [4096, 4096], P(('group', 'ep')), parts along dimension 0, may hold values from -8 to 8
- keys: bfloat16 [4096, 256], P(('group', 'ep')), parts along dimension 0, may hold values from -8 to 8
- values: bfloat16 [4096, 256], P(('group', 'ep')), parts along dimension 0, may hold values from -24 to 24
- segment_ids: int32 [4096], P(('group', 'ep')), parts along dimension 0, may hold values from 0 to 3, never falling along the last dimension, each value on 1 to 1024 neighbouring positions
- residual: bfloat16 [4096, 4096], P(('group', 'ep')), parts along dimension 0, may hold values from -6 to 6
- norm_gain: bfloat16 [4096], replicated, may hold values from 0.5 to 1.5
- route_ids: int32 [4096, 2], P(('group', 'ep')), parts along dimension 0, may hold values from 0 to 7, all different within a row; in each aligned block of 128 rows (0 to 127, 128 to 255, ...) at most 64 rows name the same one
- route_weights: float32 [4096, 2], P(('group', 'ep')), parts along dimension 0, may hold values from 0.2 to 1
- w_gate: bfloat16 [16, 4096, 384], P('ep'), may hold values from -0.09375 to 0.09375
- w_up: bfloat16 [16, 4096, 384], P('ep'), may hold values from -0.09375 to 0.09375
- w_down: bfloat16 [16, 384, 4096], P('ep'), may hold values from -0.21875 to 0.21875
Outputs:
- layer_out: bfloat16 [4096, 4096], P(('group', 'ep')), parts along dimension 0
There are 2 independent parts, one for each index of `group`. A program takes and returns all parts, laid end to end along the dimension named above; an argument that names none is the same for every part. Nothing has to cross between parts.
Inputs may be any that keep to these rules, and one draw needn't show every extreme that they name: `segment_ids`: document ids never fall along the row; a document holds 1 to 1024 tokens. `route_ids`: each token names 2 different experts; among the 128 tokens of one device no expert is named more than 64 times.
All inputs are finite; a program needn't handle non-finite values.
Results may differ from a plain program's by a relative error of at most 0.007.
Values may be sent and summed in bfloat16 or wider, within the bound.
A program may use at most 128 MiB of HBM per device.

v0:
```python
import math

import jax
import jax.numpy as jnp
from jax import lax
from jax.sharding import PartitionSpec as P

HEAD_SIZE = 128
REACH = 8


NEGATIVE = -1e30


def from_behind(x, axis, by):
    peers = lax.axis_size(axis)
    pairs = [(i, i + by) for i in range(peers) if 0 <= i + by < peers]
    return lax.ppermute(x, axis, pairs)


def expert_rows(rows, gate_half, up_half, down_half):
    gate = jnp.dot(rows, gate_half, preferred_element_type=jnp.float32)
    upward = jnp.dot(rows, up_half, preferred_element_type=jnp.float32)
    hidden = (jax.nn.silu(gate) * upward).astype(jnp.bfloat16)
    return jnp.dot(hidden, down_half, preferred_element_type=jnp.float32).astype(jnp.bfloat16)


def attend_block(state, query_tiles, key_piece, value_piece, allowed, scale):
    highest, denominator, numerator = state
    count_keys = key_piece.shape[0]
    key_tiles = key_piece.reshape(count_keys, query_tiles.shape[1], query_tiles.shape[3])
    value_tiles = value_piece.reshape(count_keys, query_tiles.shape[1], query_tiles.shape[3])
    scores = (
        jnp.einsum("tgjd,sgd->tgjs", query_tiles, key_tiles, preferred_element_type=jnp.float32)
        * scale
    )
    scores = jnp.where(allowed[:, None, None, :], scores, NEGATIVE)
    fresh = jnp.maximum(highest, jnp.max(scores, -1))
    factor = jnp.exp(highest - fresh)
    expo = jnp.exp(scores - fresh[..., None])
    denominator = denominator * factor + jnp.sum(expo, -1)
    numerator = numerator * factor[..., None] + jnp.einsum(
        "tgjs,sgd->tgjd", expo.astype(jnp.bfloat16), value_tiles, preferred_element_type=jnp.float32
    )
    return (fresh, denominator, numerator)


def local(
    queries,
    keys,
    values,
    segment_ids,
    residual,
    norm_gain,
    route_ids,
    route_weights,
    w_gate,
    w_up,
    w_down,
):
    rows = queries.shape[0]
    width = residual.shape[1]
    kv_heads = keys.shape[1] // HEAD_SIZE
    query_head_group = queries.shape[1] // (kv_heads * HEAD_SIZE)
    scale = 1.0 / math.sqrt(HEAD_SIZE)
    position = lax.axis_index("ep")
    query_tiles = queries.reshape(rows, kv_heads, query_head_group, HEAD_SIZE)
    query_seg = segment_ids.astype(jnp.float32)
    query_pos = position * rows + jnp.arange(rows, dtype=jnp.int32)
    own_seg = segment_ids.astype(jnp.bfloat16)

    def visit(state, key_piece, value_piece, seg_piece, offset):
        key_pos = (position - offset) * rows + jnp.arange(rows, dtype=jnp.int32)
        allowed = (
            (seg_piece.astype(jnp.float32)[None, :] == query_seg[:, None])
            & (key_pos[None, :] <= query_pos[:, None])
            & (key_pos[None, :] >= 0)
        )
        return attend_block(state, query_tiles, key_piece, value_piece, allowed, scale)

    state = (
        jnp.full((rows, kv_heads, query_head_group), NEGATIVE, jnp.float32),
        jnp.zeros((rows, kv_heads, query_head_group), jnp.float32),
        jnp.zeros((rows, kv_heads, query_head_group, HEAD_SIZE), jnp.float32),
    )
    state = visit(state, keys, values, own_seg, 0)
    moving = (keys, values, own_seg)
    for offset in range(1, REACH + 1):
        moving = from_behind((moving[0], moving[1], moving[2]), "ep", 1)
        state = visit(state, moving[0], moving[1], moving[2], offset)
    attended = (state[2] / state[1][..., None]).reshape(rows, width).astype(jnp.bfloat16)
    stream = (residual.astype(jnp.float32) + attended.astype(jnp.float32)).astype(jnp.bfloat16)
    stream_f = stream.astype(jnp.float32)
    normed = (
        stream_f
        * lax.rsqrt(jnp.mean(stream_f * stream_f, -1, keepdims=True) + 1e-06)
        * norm_gain.astype(jnp.float32)
    ).astype(jnp.bfloat16)
    n_experts = lax.axis_size("ep") // 2
    topk = route_ids.shape[1]
    capacity = max(2, 2 * rows * topk // n_experts)
    flat = route_ids.reshape(-1)
    onehot = (flat[:, None] == jnp.arange(n_experts, dtype=jnp.int32)[None, :]).astype(jnp.int32)
    earlier = jnp.cumsum(onehot, 0) - onehot
    slot = jnp.sum(earlier * onehot, 1)
    target = flat * capacity + slot
    source_row = (
        jnp.full((n_experts * capacity,), rows, jnp.int32)
        .at[target]
        .set(jnp.arange(rows * topk, dtype=jnp.int32) // topk)
    )
    padded = jnp.concatenate([normed, jnp.zeros((1, width), jnp.bfloat16)], 0)
    buffer = padded[source_row].reshape(n_experts, capacity, width)
    gate_half = w_gate[0]
    up_half = w_up[0]
    down_half = w_down[0]
    outgoing = jnp.repeat(buffer, 2, axis=0)
    arrived = lax.all_to_all(outgoing, "ep", split_axis=0, concat_axis=0, tiled=True)
    partial_value = expert_rows(arrived.reshape(-1, width), gate_half, up_half, down_half).reshape(
        arrived.shape
    )
    returned = lax.all_to_all(partial_value, "ep", split_axis=0, concat_axis=0, tiled=True)
    halves = returned.reshape(n_experts, 2, capacity, width).astype(jnp.float32)
    results = (halves[:, 0] + halves[:, 1]).astype(jnp.bfloat16)
    picked = results.reshape(-1, width)[target].reshape(rows, topk, width)
    mixed = jnp.sum(route_weights[:, :, None] * picked.astype(jnp.float32), 1)
    return (stream_f + mixed).astype(jnp.bfloat16)


def solution(mesh):
    placed = (
        P(("group", "ep"), None),
        P(("group", "ep"), None),
        P(("group", "ep"), None),
        P(("group", "ep")),
        P(("group", "ep"), None),
        P(),
        P(("group", "ep"), None),
        P(("group", "ep"), None),
        P("ep", None, None),
        P("ep", None, None),
        P("ep", None, None),
    )
    return jax.shard_map(
        local, mesh=mesh, in_specs=placed, out_specs=P(("group", "ep"), None), check_vma=False
    )
```

profile of v0, /device:TPU:15, one launch (start us, length us, event | category | flops | bytes accessed | tf_op | source)
XLA Modules:
  0.0 620.9 jit_solution(2271623100030963680)
XLA Ops:
  0.8 3.9 collective-permute-start
  20.3 4.7 collective-permute-start.6
  25.7 5.0 collective-permute-start.9
  31.4 5.0 collective-permute-start.12
  49.6 5.0 collective-permute-start.21
  68.1 3.8 fusion.91
  71.9 3.9 collective-permute-start.8
  88.6 3.9 fusion.89
  97.3 3.8 fusion.88
  106.5 3.8 fusion.87
  147.1 8.2 %fusion.12 = bf16[128,2,16,128]{0,3,2,1:T(8,128)(2,1)S(1)} fusion(f32[2,128,16,128]{1,3,2,0:T(8,128)} %fusion.42, f32[2,128,16,128]{1,3,2,0:T(8,128)} %fusion.44, f32[2,128,16,128]{1,3,2,0:T(8,128)} %fusion.46, f32[2,128,16,128]{1,3,2,0:T(8,128)} %fusion.48, f32[2,128,16,128]{1,3,2,0:T(8,128)} %fusion.50, f32[2,128,16,128]{1,3,2,0:T(8,128)} %fusion.52, ...), kind=kOutput, calls=%fused_computation.23 | convolution fusion | flops 145227776 | bytes 20168704 | tf_op jit(solution)/shard_map/tgjs,sgd->tgjd/dot_general | solution.py:42
  164.7 10.0 %gather_fusion = bf16[512,4096]{1,0:T(8,128)(2,1)} fusion(bf16[129,4096]{1,0:T(8,128)(2,1)} %concatenate.3, s32[1024]{0:T(1024)S(1)} %copy-done.19), kind=kCustom, calls=%fused_computation | custom fusion | bytes 8390656 | tf_op jit(solution)/shard_map/gather | solution.py:113
  174.7 6.5 %broadcast_in_dim.84 = bf16[8,2,64,4096]{3,2,1,0:T(8,128)(2,1)} broadcast(bf16[8,64,4096]{2,1,0:T(8,128)(2,1)} %bitcast.233), dimensions={0,2,3} | broadcast | bytes 12582912 | tf_op jit(solution)/shard_map/broadcast_in_dim | solution.py:117
  181.1 192.5 %all_to_all.10 = bf16[16,64,4096]{2,1,0:T(8,128)(2,1)S(1)} all-to-all(bf16[16,64,4096]{2,1,0:T(8,128)(2,1)} %bitcast.232), channel_id=1, replica_groups=mesh['group'=2,'ep'=16] {'ep'}, dimensions={0} | all-to-all | bytes 16777216 | tf_op jit(solution)/shard_map/all_to_all | solution.py:118
  373.6 4.5 fusion.5
  378.1 4.6 multiply_convert_fusion
  382.7 6.8 %convolution_convert_fusion = bf16[1024,4096]{1,0:T(8,128)(2,1)} fusion(bf16[1024,384]{1,0:T(8,128)(2,1)S(1)} %multiply_convert_fusion, bf16[1,384,4096]{2,1,0:T(8,128)(2,1)S(1)} %copy-done), kind=kOutput, calls=%fused_computation.7 | convolution fusion | flops 3225419776 | bytes 12320768 | tf_op jit(solution)/shard_map/dot_general | solution.py:25
  389.5 5.5 all-to-all-start.1
  395.2 182.1 %all-to-all-done.1 = bf16[16,64,4096]{2,1,0:T(8,128)(2,1)} async-done(((bf16[16,64,4096]{2,1,0:T(8,128)(2,1)}), bf16[16,64,4096]{2,1,0:T(8,128)(2,1)}, u32[]{:S(2)}, u32[]{:S(2)}) %all-to-all-start.1) | async-done | bytes 8388640 | tf_op jit(solution)/shard_map/all_to_all | solution.py:122
  577.2 11.4 %convert.3 = f32[8,2,64,4096]{3,2,1,0:T(8,128)} convert(bf16[8,2,64,4096]{3,2,1,0:T(8,128)(2,1)} %bitcast.75) | non-fusion elementwise | flops 4194304 | bytes 25165824 | tf_op jit(solution)/shard_map/convert_element_type | solution.py:123
  588.6 8.4 %fusion.1 = bf16[8,1,64,4096]{3,2,0,1:T(8,128)(2,1)} fusion(f32[8,2,64,4096]{3,2,1,0:T(8,128)} %convert.3), kind=kLoop, calls=%fused_computation.5 | loop fusion | flops 4194304 | bytes 20971520 | tf_op jit(solution)/shard_map/convert_element_type | solution.py:124
  597.0 7.9 %gather_fusion.1 = bf16[256,4096]{1,0:T(8,128)(2,1)} fusion(bf16[512,4096]{1,0:T(8,128)(2,1)} %bitcast.231, s32[1024]{0:T(1024)S(1)} %pad_clamp_fusion), kind=kCustom, calls=%fused_computation.1 | custom fusion | bytes 4195328 | tf_op jit(solution)/shard_map/gather | solution.py:125
  605.0 5.6 reshape.1018
  610.6 8.8 %multiply_reduce_fusion = f32[128,4096]{1,0:T(8,128)S(1)} fusion(f32[128,2,4096]{2,1,0:T(2,128)} %reshape.1018, f32[128,2]{1,0:T(8,128)S(1)} %copy.82), kind=kLoop, calls=%fused_computation.8 | loop fusion | flops 1572864 | bytes 6292480 | tf_op jit(solution)/shard_map/reduce_sum | solution.py:126
  (187 shorter events, 114.2 us)
Async XLA Ops:
  0.8 16.5 %collective-permute-start = (bf16[128]{0:T(256)(128)(2,1)S(1)}, bf16[128]{0:T(256)(128)(2,1)S(1)}, u32[]{:S(2)}, u32[]{:S(2)}) collective-permute-start(bf16[128]{0:T(256)(128)(2,1)S(1)} %get-tuple-element.37), channel_id=1, source_target_pairs={{0,1},{1,2},{2,3},{3,4},{4,5},{5,6},{6,7},{7,8},{8,9},{9,10},{10,1... | collective-permute-start | bytes 776 | tf_op jit(solution)/shard_map/ppermute | solution.py:18
  5.7 51.9 %collective-permute-start.1 = (bf16[128,256]{0,1:T(8,128)(2,1)S(1)}, bf16[128,256]{0,1:T(8,128)(2,1)S(1)}, u32[]{:S(2)}, u32[]{:S(2)}) collective-permute-start(bf16[128,256]{0,1:T(8,128)(2,1)S(1)} %copy.48), channel_id=1, source_target_pairs={{0,1},{1,2},{2,3},{3,4},{4,5},{5,6},{6,7},{7,8},{8,9},{9,10},{10,1... | collective-permute-start | bytes 196616 | tf_op jit(solution)/shard_map/ppermute | solution.py:18
  7.6 55.7 %collective-permute-start.2 = (bf16[128,256]{1,0:T(8,128)(2,1)}, bf16[128,256]{1,0:T(8,128)(2,1)}, u32[]{:S(2)}, u32[]{:S(2)}) collective-permute-start(bf16[128,256]{1,0:T(8,128)(2,1)} %param.13), channel_id=1, source_target_pairs={{0,1},{1,2},{2,3},{3,4},{4,5},{5,6},{6,7},{7,8},{8,9},{9,10},{10,1... | collective-permute-start | bytes 196616 | tf_op jit(solution)/shard_map/ppermute | solution.py:18
  20.3 5.4 collective-permute-start.6
  25.7 5.7 collective-permute-start.9
  31.4 7.4 %collective-permute-start.12 = (bf16[128]{0:T(256)(128)(2,1)S(1)}, bf16[128]{0:T(256)(128)(2,1)S(1)}, u32[]{:S(2)}, u32[]{:S(2)}) collective-permute-start(bf16[128]{0:T(256)(128)(2,1)S(1)} %collective-permute-done.9), channel_id=1, source_target_pairs={{0,1},{1,2},{2,3},{3,4},{4,5},{5,6},{6,7},{7,8},{8,9},{9,10},{10,1... | collective-permute-start | bytes 776 | tf_op jit(solution)/shard_map/ppermute | solution.py:18
  38.9 5.5 collective-permute-start.15
  44.3 4.3 collective-permute-start.18
  49.6 7.7 %collective-permute-start.21 = (bf16[128]{0:T(256)(128)(2,1)S(1)}, bf16[128]{0:T(256)(128)(2,1)S(1)}, u32[]{:S(2)}, u32[]{:S(2)}) collective-permute-start(bf16[128]{0:T(256)(128)(2,1)S(1)} %collective-permute-done.18), channel_id=1, source_target_pairs={{0,1},{1,2},{2,3},{3,4},{4,5},{5,6},{6,7},{7,8},{8,9},{9,10},{10,1... | collective-permute-start | bytes 776 | tf_op jit(solution)/shard_map/ppermute | solution.py:18
  57.5 8.6 %collective-permute-start.4 = (bf16[128,256]{0,1:T(8,128)(2,1)S(1)}, bf16[128,256]{0,1:T(8,128)(2,1)}, u32[]{:S(2)}, u32[]{:S(2)}) collective-permute-start(bf16[128,256]{0,1:T(8,128)(2,1)S(1)} %collective-permute-done.1), channel_id=1, source_target_pairs={{0,1},{1,2},{2,3},{3,4},{4,5},{5,6},{6,7},{7,8},{8,9},{9,10},{10,1... | collective-permute-start | bytes 196616 | tf_op jit(solution)/shard_map/ppermute | solution.py:18
  63.3 8.7 %collective-permute-start.5 = (bf16[128,256]{1,0:T(8,128)(2,1)}, bf16[128,256]{1,0:T(8,128)(2,1)}, u32[]{:S(2)}, u32[]{:S(2)}) collective-permute-start(bf16[128,256]{1,0:T(8,128)(2,1)} %collective-permute-done.2), channel_id=1, source_target_pairs={{0,1},{1,2},{2,3},{3,4},{4,5},{5,6},{6,7},{7,8},{8,9},{9,10},{10,1... | collective-permute-start | bytes 196616 | tf_op jit(solution)/shard_map/ppermute | solution.py:18
  66.2 10.7 %collective-permute-start.7 = (bf16[128,256]{0,1:T(8,128)(2,1)}, bf16[128,256]{0,1:T(8,128)(2,1)S(1)}, u32[]{:S(2)}, u32[]{:S(2)}) collective-permute-start(bf16[128,256]{0,1:T(8,128)(2,1)} %collective-permute-done.4), channel_id=1, source_target_pairs={{0,1},{1,2},{2,3},{3,4},{4,5},{5,6},{6,7},{7,8},{8,9},{9,10},{10,1... | collective-permute-start | bytes 196616 | tf_op jit(solution)/shard_map/ppermute | solution.py:18
  71.9 11.8 %collective-permute-start.8 = (bf16[128,256]{1,0:T(8,128)(2,1)}, bf16[128,256]{1,0:T(8,128)(2,1)}, u32[]{:S(2)}, u32[]{:S(2)}) collective-permute-start(bf16[128,256]{1,0:T(8,128)(2,1)} %collective-permute-done.5), channel_id=1, source_target_pairs={{0,1},{1,2},{2,3},{3,4},{4,5},{5,6},{6,7},{7,8},{8,9},{9,10},{10,1... | collective-permute-start | bytes 196616 | tf_op jit(solution)/shard_map/ppermute | solution.py:18
  76.8 9.8 %collective-permute-start.10 = (bf16[128,256]{0,1:T(8,128)(2,1)S(1)}, bf16[128,256]{0,1:T(8,128)(2,1)}, u32[]{:S(2)}, u32[]{:S(2)}) collective-permute-start(bf16[128,256]{0,1:T(8,128)(2,1)S(1)} %collective-permute-done.7), channel_id=1, source_target_pairs={{0,1},{1,2},{2,3},{3,4},{4,5},{5,6},{6,7},{7,8},{8,9},{9,10},{10,1... | collective-permute-start | bytes 196616 | tf_op jit(solution)/shard_map/ppermute | solution.py:18
  83.8 8.7 %collective-permute-start.11 = (bf16[128,256]{1,0:T(8,128)(2,1)}, bf16[128,256]{1,0:T(8,128)(2,1)}, u32[]{:S(2)}, u32[]{:S(2)}) collective-permute-start(bf16[128,256]{1,0:T(8,128)(2,1)} %collective-permute-done.8), channel_id=1, source_target_pairs={{0,1},{1,2},{2,3},{3,4},{4,5},{5,6},{6,7},{7,8},{8,9},{9,10},{10,1... | collective-permute-start | bytes 196616 | tf_op jit(solution)/shard_map/ppermute | solution.py:18
  86.7 8.7 %collective-permute-start.13 = (bf16[128,256]{0,1:T(8,128)(2,1)}, bf16[128,256]{0,1:T(8,128)(2,1)}, u32[]{:S(2)}, u32[]{:S(2)}) collective-permute-start(bf16[128,256]{0,1:T(8,128)(2,1)} %collective-permute-done.10), channel_id=1, source_target_pairs={{0,1},{1,2},{2,3},{3,4},{4,5},{5,6},{6,7},{7,8},{8,9},{9,10},{10,1... | collective-permute-start | bytes 196616 | tf_op jit(solution)/shard_map/ppermute | solution.py:18
  92.5 8.7 %collective-permute-start.14 = (bf16[128,256]{1,0:T(8,128)(2,1)}, bf16[128,256]{1,0:T(8,128)(2,1)}, u32[]{:S(2)}, u32[]{:S(2)}) collective-permute-start(bf16[128,256]{1,0:T(8,128)(2,1)} %collective-permute-done.11), channel_id=1, source_target_pairs={{0,1},{1,2},{2,3},{3,4},{4,5},{5,6},{6,7},{7,8},{8,9},{9,10},{10,1... | collective-permute-start | bytes 196616 | tf_op jit(solution)/shard_map/ppermute | solution.py:18
  95.4 9.2 %collective-permute-start.16 = (bf16[128,256]{0,1:T(8,128)(2,1)}, bf16[128,256]{0,1:T(8,128)(2,1)}, u32[]{:S(2)}, u32[]{:S(2)}) collective-permute-start(bf16[128,256]{0,1:T(8,128)(2,1)} %collective-permute-done.13), channel_id=1, source_target_pairs={{0,1},{1,2},{2,3},{3,4},{4,5},{5,6},{6,7},{7,8},{8,9},{9,10},{10,1... | collective-permute-start | bytes 196616 | tf_op jit(solution)/shard_map/ppermute | solution.py:18
  102.7 7.7 %collective-permute-start.17 = (bf16[128,256]{1,0:T(8,128)(2,1)}, bf16[128,256]{1,0:T(8,128)(2,1)}, u32[]{:S(2)}, u32[]{:S(2)}) collective-permute-start(bf16[128,256]{1,0:T(8,128)(2,1)} %collective-permute-done.14), channel_id=1, source_target_pairs={{0,1},{1,2},{2,3},{3,4},{4,5},{5,6},{6,7},{7,8},{8,9},{9,10},{10,1... | collective-permute-start | bytes 196616 | tf_op jit(solution)/shard_map/ppermute | solution.py:18
  104.6 8.6 %collective-permute-start.19 = (bf16[128,256]{0,1:T(8,128)(2,1)}, bf16[128,256]{0,1:T(8,128)(2,1)}, u32[]{:S(2)}, u32[]{:S(2)}) collective-permute-start(bf16[128,256]{0,1:T(8,128)(2,1)} %collective-permute-done.16), channel_id=1, source_target_pairs={{0,1},{1,2},{2,3},{3,4},{4,5},{5,6},{6,7},{7,8},{8,9},{9,10},{10,1... | collective-permute-start | bytes 196616 | tf_op jit(solution)/shard_map/ppermute | solution.py:18
  111.3 7.7 %collective-permute-start.20 = (bf16[128,256]{1,0:T(8,128)(2,1)}, bf16[128,256]{1,0:T(8,128)(2,1)}, u32[]{:S(2)}, u32[]{:S(2)}) collective-permute-start(bf16[128,256]{1,0:T(8,128)(2,1)} %collective-permute-done.17), channel_id=1, source_target_pairs={{0,1},{1,2},{2,3},{3,4},{4,5},{5,6},{6,7},{7,8},{8,9},{9,10},{10,1... | collective-permute-start | bytes 196616 | tf_op jit(solution)/shard_map/ppermute | solution.py:18
  113.3 9.6 %collective-permute-start.22 = (bf16[128,256]{0,1:T(8,128)(2,1)}, bf16[128,256]{0,1:T(8,128)(2,1)}, u32[]{:S(2)}, u32[]{:S(2)}) collective-permute-start(bf16[128,256]{0,1:T(8,128)(2,1)} %collective-permute-done.19), channel_id=1, source_target_pairs={{0,1},{1,2},{2,3},{3,4},{4,5},{5,6},{6,7},{7,8},{8,9},{9,10},{10,1... | collective-permute-start | bytes 196616 | tf_op jit(solution)/shard_map/ppermute | solution.py:18
  120.6 25.6 %collective-permute-start.23 = (bf16[128,256]{1,0:T(8,128)(2,1)}, bf16[128,256]{1,0:T(8,128)(2,1)}, u32[]{:S(2)}, u32[]{:S(2)}) collective-permute-start(bf16[128,256]{1,0:T(8,128)(2,1)} %collective-permute-done.20), channel_id=1, source_target_pairs={{0,1},{1,2},{2,3},{3,4},{4,5},{5,6},{6,7},{7,8},{8,9},{9,10},{10,1... | collective-permute-start | bytes 196616 | tf_op jit(solution)/shard_map/ppermute | solution.py:18
  389.5 187.7 %all-to-all-start.1 = ((bf16[16,64,4096]{2,1,0:T(8,128)(2,1)}), bf16[16,64,4096]{2,1,0:T(8,128)(2,1)}, u32[]{:S(2)}, u32[]{:S(2)}) async-start(bf16[16,64,4096]{2,1,0:T(8,128)(2,1)} %bitcast.234), calls=%async_computation.1 | async-start | bytes 16777216 | tf_op jit(solution)/shard_map/all_to_all | solution.py:122
  (31 other events, 771.1 us)
where the time goes:
time: 631 us; the launch traced here: 621 us
  blocking collectives  192 us (30%)
  waiting for transfers between devices  184 us (29%)
  starting transfers between devices  75.1 us (12%)
  matrix products  68.3 us (11%)
  local copies, waits for them, and re-layouts  53.8 us (9%)
  other arithmetic  46 us (7%)
    all_to_all x1, blocking collectives, local(): lax.all_to_all(outgoing, 'ep', split_axis=0, concat_axis=0, tiled=True)  192 us
    all_to_all x1, waiting for transfers between devices, local(): lax.all_to_all(partial_value, 'ep', split_axis=0, concat_axis=0, tiled=True)  182 us
    ppermute x24, starting transfers between devices, from_behind(): return lax.ppermute(x, axis, pairs)  69.6 us
    dot_general x9, matrix products, attend_block(): jnp.einsum('tgjd,sgd->tgjs', query_tiles, key_tiles, preferred_element_ty...  30.1 us
    dot_general x9, matrix products, attend_block(): jnp.einsum('tgjs,sgd->tgjd', expo.astype(jnp.bfloat16), value_tiles, pref...  22.5 us
  transfers between devices with their start and end apart: 25, of which 5 were waited for; matrix products, arithmetic and copies ran while one was open for 11% of the time, Pallas kernels for 0%

commit v1 on v0

v1 whole, which is shorter than its diff:
```python
import functools
import math

import jax
import jax.numpy as jnp
from jax import lax
from jax.experimental import pallas as pl
from jax.experimental.pallas import tpu as pltpu
from jax.sharding import PartitionSpec as P

HEAD_SIZE = 128
REACH = 8
NEGATIVE = -1e30
MESH = pl.DeviceIdType.MESH
SEG_ROWS = 16


def nt_dot(a, b):
    return lax.dot_general(a, b, (((1,), (1,)), ((), ())), preferred_element_type=jnp.float32)


def attention_kernel(
    n, kv_heads, q_ref, kv_ref, segcol_ref, res_ref, gain_ref, place_ref,
    stream_ref, rows_ref,
    held, bias, attended, normed, send_sem, recv_sem,
):
    me = lax.axis_index("ep")
    rows = q_ref.shape[0]
    heads = q_ref.shape[1] // HEAD_SIZE
    per_kv = heads // kv_heads
    kv_width = kv_heads * HEAD_SIZE
    span = rows + SEG_ROWS
    reach = min(REACH, n - 1)

    barrier = pltpu.get_barrier_semaphore()
    for d in range(1, reach + 1):
        pl.semaphore_signal(
            barrier, inc=1, device_id={"ep": lax.rem(me + n - d, n)}, device_id_type=MESH
        )
    pl.semaphore_wait(barrier, reach)

    copies = []
    for d in range(1, reach + 1):
        copy = pltpu.make_async_remote_copy(
            src_ref=kv_ref, dst_ref=held.at[d],
            send_sem=send_sem.at[d], recv_sem=recv_sem.at[d],
            device_id={"ep": lax.rem(me + d, n)}, device_id_type=MESH,
        )
        copy.start()
        copies.append(copy)
    held[0] = kv_ref[...]
    for copy in copies:
        copy.wait()

    query_seg = segcol_ref[...]
    t = lax.broadcasted_iota(jnp.int32, (rows, rows), 0)
    u = lax.broadcasted_iota(jnp.int32, (rows, rows), 1)
    for d in range(reach + 1):
        key_seg = held[d, rows : rows + SEG_ROWS, 0:rows][0:1].astype(jnp.float32)
        allowed = (key_seg == query_seg) & (u - d * rows <= t) & (u + (me - d) * rows >= 0)
        bias[:, d * rows : (d + 1) * rows] = jnp.where(allowed, 0.0, NEGATIVE)

    scale = math.log2(math.e) / math.sqrt(HEAD_SIZE)

    def one_head(h, g):
        col = pl.multiple_of(h * HEAD_SIZE, HEAD_SIZE)
        q = q_ref[:, pl.ds(col, HEAD_SIZE)]
        k = jnp.concatenate(
            [held[d, 0:rows, g * HEAD_SIZE : (g + 1) * HEAD_SIZE] for d in range(reach + 1)], 0
        )
        v = jnp.concatenate(
            [
                held[d, 0:rows, kv_width + g * HEAD_SIZE : kv_width + (g + 1) * HEAD_SIZE]
                for d in range(reach + 1)
            ],
            0,
        )
        s = nt_dot(q, k) * scale + bias[...]
        top = jnp.max(s, -1, keepdims=True)
        p = jnp.exp2(s - top)
        total = jnp.sum(p, -1, keepdims=True)
        pv = jnp.dot(p.astype(jnp.bfloat16), v, preferred_element_type=jnp.float32)
        attended[:, pl.ds(col, HEAD_SIZE)] = (pv / total).astype(jnp.bfloat16)

    def heads_step(i, carry):
        for g in range(kv_heads):
            one_head(i + g * per_kv, g)
        return carry

    lax.fori_loop(0, per_kv, heads_step, 0)

    chunk = 16

    def norm_step(i, carry):
        r = pl.ds(pl.multiple_of(i * chunk, chunk), chunk)
        stream = (res_ref[r, :].astype(jnp.float32) + attended[r, :].astype(jnp.float32)).astype(
            jnp.bfloat16
        )
        stream_ref[r, :] = stream
        sf = stream.astype(jnp.float32)
        inv = lax.rsqrt(jnp.mean(sf * sf, -1, keepdims=True) + 1e-06)
        normed[r, :] = (sf * inv * gain_ref[...].astype(jnp.float32)).astype(jnp.bfloat16)
        return carry

    lax.fori_loop(0, rows // chunk, norm_step, 0)

    tile = 512

    def place_step(i, carry):
        c = pl.ds(pl.multiple_of(i * tile, tile), tile)
        rows_ref[:, c] = jnp.dot(
            place_ref[...], normed[:, c], preferred_element_type=jnp.float32
        ).astype(jnp.bfloat16)
        return carry

    lax.fori_loop(0, normed.shape[1] // tile, place_step, 0)


def attention(n, kv_heads, queries, kv, segcol, residual, gain, place):
    rows, width = queries.shape
    reach = min(REACH, n - 1)
    vmem = pl.BlockSpec(memory_space=pltpu.VMEM)
    return pl.pallas_call(
        functools.partial(attention_kernel, n, kv_heads),
        out_shape=(
            jax.ShapeDtypeStruct((rows, width), jnp.bfloat16),
            jax.ShapeDtypeStruct((place.shape[0], width), jnp.bfloat16),
        ),
        in_specs=[vmem] * 6,
        out_specs=(vmem, vmem),
        scratch_shapes=[
            pltpu.VMEM((reach + 1,) + kv.shape, jnp.bfloat16),
            pltpu.VMEM((rows, (reach + 1) * rows), jnp.float32),
            pltpu.VMEM((rows, width), jnp.bfloat16),
            pltpu.VMEM((rows, width), jnp.bfloat16),
            pltpu.SemaphoreType.DMA((reach + 1,)),
            pltpu.SemaphoreType.DMA((reach + 1,)),
        ],
        compiler_params=pltpu.CompilerParams(
            collective_id=0, has_side_effects=True, vmem_limit_bytes=40 * 1024 * 1024
        ),
        name="attention",
    )(queries, kv, segcol, residual, gain, place)


def local(
    queries, keys, values, segment_ids, residual, norm_gain, route_ids, route_weights,
    w_gate, w_up, w_down,
):
    rows, width = residual.shape
    n = lax.axis_size("ep")
    kv_heads = keys.shape[1] // HEAD_SIZE
    n_experts = n // 2
    topk = route_ids.shape[1]
    capacity = max(2, 2 * rows * topk // n_experts)

    swap = [(i, i ^ 1) for i in range(n)]
    core = lax.rem(lax.axis_index("ep"), 2)
    other_gate = lax.ppermute(w_gate[0], "ep", swap)
    other_up = lax.ppermute(w_up[0], "ep", swap)
    other_down = lax.ppermute(w_down[0], "ep", swap)

    seg_row = jnp.zeros((SEG_ROWS, 2 * keys.shape[1]), jnp.bfloat16)
    seg_row = lax.dynamic_update_slice(
        seg_row, jnp.broadcast_to(segment_ids.astype(jnp.bfloat16)[None, :], (SEG_ROWS, rows)), (0, 0)
    )
    kv = jnp.concatenate([jnp.concatenate([keys, values], 1), seg_row], 0)
    segcol = segment_ids.astype(jnp.float32)[:, None]

    experts = jnp.arange(n_experts, dtype=jnp.int32)
    hit = route_ids[:, :, None] == experts[None, None, :]
    named = jnp.any(hit, 1)
    weight = jnp.sum(jnp.where(hit, route_weights[:, :, None], 0.0), 1)
    below = jnp.tril(jnp.ones((rows, rows), jnp.bfloat16), -1)
    slot = jnp.dot(below, named.astype(jnp.bfloat16), preferred_element_type=jnp.float32).astype(jnp.int32)
    code = jnp.where(named, slot, -1)
    slots = jnp.arange(capacity, dtype=jnp.int32)
    place = (code.T[:, None, :] == slots[None, :, None]).astype(jnp.bfloat16)
    place = place.reshape(n_experts * capacity, rows)
    mix = jnp.where(code[:, :, None] == slots[None, None, :], weight[:, :, None], 0.0)
    mix = mix.reshape(rows, n_experts * capacity)
    mix_hi = mix.astype(jnp.bfloat16)
    mix_lo = (mix - mix_hi.astype(jnp.float32)).astype(jnp.bfloat16)

    stream, outgoing = attention(n, kv_heads, queries, kv, segcol, residual, norm_gain[None, :], place)

    groups = [[c for c in range(k, n, 2)] for k in range(2)]
    arrived = lax.all_to_all(
        outgoing.reshape(n_experts, capacity, width), "ep", split_axis=0, concat_axis=0,
        axis_index_groups=groups, tiled=True,
    ).reshape(-1, width)

    def half(gate_half, up_half, down_half):
        gate = jnp.dot(arrived, gate_half, preferred_element_type=jnp.float32)
        upward = jnp.dot(arrived, up_half, preferred_element_type=jnp.float32)
        hidden = (jax.nn.silu(gate) * upward).astype(jnp.bfloat16)
        return jnp.dot(hidden, down_half, preferred_element_type=jnp.float32)

    out = half(w_gate[0], w_up[0], w_down[0]) + half(other_gate, other_up, other_down)
    returned = lax.all_to_all(
        out.astype(jnp.bfloat16).reshape(n_experts, capacity, width), "ep", split_axis=0,
        concat_axis=0, axis_index_groups=groups, tiled=True,
    ).reshape(-1, width)
    mixed = jnp.dot(mix_hi, returned, preferred_element_type=jnp.float32) + jnp.dot(
        mix_lo, returned, preferred_element_type=jnp.float32
    )
    return (stream.astype(jnp.float32) + mixed).astype(jnp.bfloat16)


def solution(mesh):
    tokens = P(("group", "ep"), None)
    split = P("ep", None, None)
    placed = (
        tokens, tokens, tokens, P(("group", "ep")), tokens, P(), tokens, tokens, split, split, split,
    )
    return jax.shard_map(local, mesh=mesh, in_specs=placed, out_specs=tokens, check_vma=False)
```

time: 631 us -> 308 us (0.49)
  the two profiles are of different devices: /device:TPU:15 before, /device:TPU:0 now
where the time goes in v1:
time: 308 us; the launch traced here: 307 us
  waiting for transfers between devices  187 us (61%)
  Pallas kernels  53.6 us (17%)
  matrix products  42.9 us (14%)
  starting transfers between devices  16.4 us (5%)
  local copies, waits for them, and re-layouts  5.29 us (2%)
    all_to_all x1, waiting for transfers between devices, local(): lax.all_to_all(out.astype(jnp.bfloat16).reshape(n_experts, capacity, widt...  93.4 us
    all_to_all x1, waiting for transfers between devices, local(): lax.all_to_all(outgoing.reshape(n_experts, capacity, width), 'ep', split_...  93.2 us
    pallas_call x1, Pallas kernels, attention(): pl.pallas_call(functools.partial(attention_kernel, n, kv_heads), out_shap...  53.6 us
    dot_general x2, matrix products, half(): return jnp.dot(hidden, down_half, preferred_element_type=jnp.float32)  24.7 us
    dot_general x2, matrix products, half(): gate = jnp.dot(arrived, gate_half, preferred_element_type=jnp.float32)  11 us
    all_to_all x1, starting transfers between devices, local(): lax.all_to_all(outgoing.reshape(n_experts, capacity, width), 'ep', split_...  10.7 us
  transfers between devices with their start and end apart: 5, of which 2 were waited for; matrix products, arithmetic and copies ran while one was open for 7% of the time, Pallas kernels for 0%

profile of v1, /device:TPU:0, one launch (start us, length us, event | category | flops | bytes accessed | tf_op | source)
XLA Modules:
  0.0 307.5 jit_solution(841097438399415726)
XLA Ops:
  0.0 0.7 fusion.27
  0.7 0.1 eq.55
  0.8 0.7 convert_bitcast_fusion
  1.5 0.1 copy.15.segcol_ref
  1.6 0.7 broadcast_in_dim.55.gain_ref
  2.3 0.2 fusion.5
  2.5 0.2 fusion.14.place_ref
  2.7 0.9 pad_maximum_fusion.kv_ref
  3.6 1.2 copy-done.1
  4.8 1.2 copy-done.2
  6.1 53.6 %attention.1 = (bf16[128,4096]{1,0:T(8,128)(2,1)S(1)}, bf16[512,4096]{1,0:T(8,128)(2,1)S(1)}) custom-call(bf16[128,4096]{1,0:T(8,128)(2,1)S(1)} %copy-done.1, bf16[144,512]{1,0:T(8,128)(2,1)S(1)} %pad_maximum_fusion.kv_ref, f32[128,1]{1,0:T(8,128)S(1)} %copy.15.segcol_ref, bf16[128,4096]{1,0:T(8,128)(2,1)S(1)} %copy-done.2, ...), custom_call_target="tpu_custom_call" | custom-call | tf_op jit(solution)/shard_map/attention/pallas_call | solution.py:123
  59.6 1.9 copy-done
  61.6 10.7 %all-to-all-start = ((bf16[8,64,4096]{2,1,0:T(8,128)(2,1)}), bf16[8,64,4096]{2,1,0:T(8,128)(2,1)}, u32[]{:S(2)}, u32[]{:S(2)}) async-start(bf16[8,64,4096]{2,1,0:T(8,128)(2,1)} %bitcast.40), calls=%async_computation | async-start | bytes 8388608 | tf_op jit(solution)/shard_map/all_to_all | solution.py:188
  72.3 0.6 collective-permute-start
  72.9 0.4 collective-permute-start.2
  73.3 93.2 %all-to-all-done = bf16[8,64,4096]{2,1,0:T(8,128)(2,1)} async-done(((bf16[8,64,4096]{2,1,0:T(8,128)(2,1)}), bf16[8,64,4096]{2,1,0:T(8,128)(2,1)}, u32[]{:S(2)}, u32[]{:S(2)}) %all-to-all-start) | async-done | bytes 4194336 | tf_op jit(solution)/shard_map/all_to_all | solution.py:188
  166.6 5.5 %fusion.31 = f32[512,384]{1,0:T(8,128)S(1)} fusion(bf16[512,4096]{1,0:T(8,128)(2,1)} %bitcast.4, bf16[1,4096,384]{2,1,0:T(8,128)(2,1)} %param.19), kind=kOutput, calls=%fused_computation.44 | convolution fusion | flops 1610612736 | bytes 8126464 | tf_op jit(solution)/shard_map/dot_general | solution.py:194
  172.1 5.5 %fusion.41 = f32[512,384]{1,0:T(8,128)S(1)} fusion(bf16[512,4096]{1,0:T(8,128)(2,1)} %bitcast.4, bf16[4096,384]{1,0:T(8,128)(2,1)} %collective-permute-done), kind=kOutput, calls=%fused_computation.53 | convolution fusion | flops 1610612736 | bytes 8126464 | tf_op jit(solution)/shard_map/dot_general | solution.py:194
  177.6 11.8 %fusion.4 = f32[512,4096]{1,0:T(8,128)} fusion(bf16[512,4096]{1,0:T(8,128)(2,1)} %bitcast.4, f32[512,384]{1,0:T(8,128)S(1)} %fusion.31, bf16[1,384,4096]{2,1,0:T(8,128)(2,1)} %param.21, bf16[1,4096,384]{2,1,0:T(8,128)(2,1)} %param.20), kind=kOutput, calls=%fused_computation.8 | convolution fusion | flops 3222405120 | bytes 19660800 | tf_op jit(solution)/shard_map/dot_general | solution.py:197
  189.4 12.9 %add_convert_fusion = bf16[512,4096]{1,0:T(8,128)(2,1)} fusion(f32[512,4096]{1,0:T(8,128)} %fusion.4, bf16[384,4096]{1,0:T(8,128)(2,1)} %collective-permute-done.2, f32[512,384]{1,0:T(8,128)S(1)} %fusion.41, bf16[512,4096]{1,0:T(8,128)(2,1)} %bitcast.4, bf16[4096,384]{1,0:T(8,128)(2,1)} %collective-permute-done.1), kind=kOutput, calls=%fused_computation | convolution fusion | flops 3226599424 | bytes 23855104 | tf_op jit(solution)/shard_map/dot_general | solution.py:197
  202.3 4.7 %all-to-all-start.1 = ((bf16[8,64,4096]{2,1,0:T(8,128)(2,1)}), bf16[8,64,4096]{2,1,0:T(8,128)(2,1)}, u32[]{:S(2)}, u32[]{:S(2)}) async-start(bf16[8,64,4096]{2,1,0:T(8,128)(2,1)} %bitcast.41), calls=%async_computation.1 | async-start | bytes 8388608 | tf_op jit(solution)/shard_map/all_to_all | solution.py:200
  207.0 93.4 %all-to-all-done.1 = bf16[8,64,4096]{2,1,0:T(8,128)(2,1)} async-done(((bf16[8,64,4096]{2,1,0:T(8,128)(2,1)}), bf16[8,64,4096]{2,1,0:T(8,128)(2,1)}, u32[]{:S(2)}, u32[]{:S(2)}) %all-to-all-start.1) | async-done | bytes 4194336 | tf_op jit(solution)/shard_map/all_to_all | solution.py:200
  300.4 2.9 convolution_bitcast_fusion
  303.3 4.1 %fusion.2 = bf16[128,4096]{1,0:T(8,128)(2,1)} fusion(f32[128,4096]{1,0:T(8,128)S(1)} %convolution_bitcast_fusion, bf16[8,64,4096]{2,1,0:T(8,128)(2,1)} %all-to-all-done.1, bf16[128,4096]{1,0:T(8,128)(2,1)S(1)} %get-tuple-element.7, f32[128,8]{0,1:T(8,128)S(1)} %select_reduce_fusion, s32[128,8]{0,1:T(8,128)S(1)} %fusion.5), kind=kOutput, calls=%fused_computation.5 | convolution fusion | flops 539099136 | bytes 8396800 | tf_op jit(solution)/shard_map/dot_general | solution.py:204
  (16 shorter events, 0.1 us)
Async XLA Ops:
  3.6 1.2 copy-start.1
  4.8 1.2 copy-start.2
  59.6 1.9 copy-start
  61.6 105.0 %all-to-all-start = ((bf16[8,64,4096]{2,1,0:T(8,128)(2,1)}), bf16[8,64,4096]{2,1,0:T(8,128)(2,1)}, u32[]{:S(2)}, u32[]{:S(2)}) async-start(bf16[8,64,4096]{2,1,0:T(8,128)(2,1)} %bitcast.40), calls=%async_computation | async-start | bytes 8388608 | tf_op jit(solution)/shard_map/all_to_all | solution.py:188
  72.3 99.8 %collective-permute-start = (bf16[4096,384]{1,0:T(8,128)(2,1)}, bf16[4096,384]{1,0:T(8,128)(2,1)}, u32[]{:S(2)}, u32[]{:S(2)}) collective-permute-start(bf16[4096,384]{1,0:T(8,128)(2,1)} %bitcast.43), channel_id=1, source_target_pairs={{0,1},{1,0},{2,3},{3,2},{4,5},{5,4},{6,7},{7,6},{8,9},{9,8},{10,11... | collective-permute-start | bytes 9437192 | tf_op jit(solution)/shard_map/ppermute | solution.py:159
  72.8 116.6 %collective-permute-start.1 = (bf16[4096,384]{1,0:T(8,128)(2,1)}, bf16[4096,384]{1,0:T(8,128)(2,1)}, u32[]{:S(2)}, u32[]{:S(2)}) collective-permute-start(bf16[4096,384]{1,0:T(8,128)(2,1)} %bitcast.44), channel_id=1, source_target_pairs={{0,1},{1,0},{2,3},{3,2},{4,5},{5,4},{6,7},{7,6},{8,9},{9,8},{10,11... | collective-permute-start | bytes 9437192 | tf_op jit(solution)/shard_map/ppermute | solution.py:160
  72.9 116.5 %collective-permute-start.2 = (bf16[384,4096]{1,0:T(8,128)(2,1)}, bf16[384,4096]{1,0:T(8,128)(2,1)}, u32[]{:S(2)}, u32[]{:S(2)}) collective-permute-start(bf16[384,4096]{1,0:T(8,128)(2,1)} %bitcast.45), channel_id=1, source_target_pairs={{0,1},{1,0},{2,3},{3,2},{4,5},{5,4},{6,7},{7,6},{8,9},{9,8},{10,11... | collective-permute-start | bytes 9437192 | tf_op jit(solution)/shard_map/ppermute | solution.py:161
  202.3 4.7 %copy-start.3 = (s32[128,2]{0,1:T(2,128)S(1)}, s32[128,2]{0,1:T(2,128)}, u32[]{:S(2)}) copy-start(s32[128,2]{0,1:T(2,128)} %param.17) | copy-start | bytes 3076
  202.3 4.7 %copy-start.4 = (f32[128,2]{0,1:T(2,128)S(1)}, f32[128,2]{0,1:T(2,128)}, u32[]{:S(2)}) copy-start(f32[128,2]{0,1:T(2,128)} %param.18) | copy-start | bytes 3076
  202.3 98.1 %all-to-all-start.1 = ((bf16[8,64,4096]{2,1,0:T(8,128)(2,1)}), bf16[8,64,4096]{2,1,0:T(8,128)(2,1)}, u32[]{:S(2)}, u32[]{:S(2)}) async-start(bf16[8,64,4096]{2,1,0:T(8,128)(2,1)} %bitcast.41), calls=%async_computation.1 | async-start | bytes 8388608 | tf_op jit(solution)/shard_map/all_to_all | solution.py:200

commit v2 on v1

--- a/solution.py
+++ b/solution.py
@@ -20,10 +20,12 @@
 
 
 def attention_kernel(
-    n, kv_heads, q_ref, kv_ref, segcol_ref, res_ref, gain_ref, place_ref,
-    stream_ref, rows_ref,
-    held, bias, attended, normed, send_sem, recv_sem,
+    n, kv_heads, placing, q_ref, kv_ref, segcol_ref, res_ref, gain_ref, *rest
 ):
+    if placing:
+        place_ref, stream_ref, rows_ref, held, bias, attended, normed, send_sem, recv_sem = rest
+    else:
+        stream_ref, normed, held, bias, attended, send_sem, recv_sem = rest
     me = lax.axis_index("ep")
     rows = q_ref.shape[0]
     heads = q_ref.shape[1] // HEAD_SIZE
@@ -104,6 +106,8 @@
 
     lax.fori_loop(0, rows // chunk, norm_step, 0)
 
+    if not placing:
+        return
     tile = 512
 
     def place_step(i, carry):
@@ -116,23 +120,29 @@
     lax.fori_loop(0, normed.shape[1] // tile, place_step, 0)
 
 
-def attention(n, kv_heads, queries, kv, segcol, residual, gain, place):
+def attention(n, kv_heads, queries, kv, segcol, residual, gain, place=None):
     rows, width = queries.shape
     reach = min(REACH, n - 1)
     vmem = pl.BlockSpec(memory_space=pltpu.VMEM)
+    placing = place is not None
+    sent = place.shape[0] if placing else rows
+    operands = (queries, kv, segcol, residual, gain) + ((place,) if placing else ())
+    scratch = [
+        pltpu.VMEM((reach + 1,) + kv.shape, jnp.bfloat16),
+        pltpu.VMEM((rows, (reach + 1) * rows), jnp.float32),
+        pltpu.VMEM((rows, width), jnp.bfloat16),
+    ]
+    if placing:
+        scratch.append(pltpu.VMEM((rows, width), jnp.bfloat16))
     return pl.pallas_call(
-        functools.partial(attention_kernel, n, kv_heads),
+        functools.partial(attention_kernel, n, kv_heads, placing),
         out_shape=(
             jax.ShapeDtypeStruct((rows, width), jnp.bfloat16),
-            jax.ShapeDtypeStruct((place.shape[0], width), jnp.bfloat16),
+            jax.ShapeDtypeStruct((sent, width), jnp.bfloat16),
         ),
-        in_specs=[vmem] * 6,
+        in_specs=[vmem] * len(operands),
         out_specs=(vmem, vmem),
-        scratch_shapes=[
-            pltpu.VMEM((reach + 1,) + kv.shape, jnp.bfloat16),
-            pltpu.VMEM((rows, (reach + 1) * rows), jnp.float32),
-            pltpu.VMEM((rows, width), jnp.bfloat16),
-            pltpu.VMEM((rows, width), jnp.bfloat16),
+        scratch_shapes=scratch + [
             pltpu.SemaphoreType.DMA((reach + 1,)),
             pltpu.SemaphoreType.DMA((reach + 1,)),
         ],
@@ -140,7 +150,244 @@
             collective_id=0, has_side_effects=True, vmem_limit_bytes=40 * 1024 * 1024
         ),
         name="attention",
-    )(queries, kv, segcol, residual, gain, place)
+    )(*operands)
+
+
+def experts_kernel(
+    n, capacity, tokens_ref, stream_ref, codes_ref, hi_ref, lo_ref,
+    gate0, up0, down0, gate1, up1, down1,
+    out_ref,
+    line, x_out, x_in, feed, hidden, result, returned, w_gate, w_up, w_down,
+    w_sem, recv_sem, up_sem, down_sem, x_send, x_recv, back_send, back_recv,
+):
+    planes = n // 4
+    n_experts = n // 2
+    last = planes - 1
+    me = lax.axis_index("ep")
+    z = me // 4
+    x = lax.rem(me // 2, 2)
+    c = lax.rem(me, 2)
+    expert = me // 2
+    partner = me + 2 - 4 * x
+    partner_expert = expert + 1 - 2 * x
+    rows, width = tokens_ref.shape
+    ffe = down0.shape[0]
+
+    barrier = pltpu.get_barrier_semaphore()
+    for k in range(1, n_experts):
+        pl.semaphore_signal(
+            barrier, inc=1, device_id={"ep": lax.rem(me + 2 * k, n)}, device_id_type=MESH
+        )
+
+    loads = []
+    for j, (g, u, d) in enumerate(((gate0, up0, down0), (gate1, up1, down1))):
+        part = pl.ds(j * ffe, ffe)
+        for k, (src, dst) in enumerate(
+            ((g, w_gate.at[:, part]), (u, w_up.at[:, part]), (d, w_down.at[part, :]))
+        ):
+            load = pltpu.make_async_copy(src, dst, w_sem.at[3 * j + k])
+            load.start()
+            loads.append(load)
+
+    line[z] = tokens_ref[...]
+    pl.semaphore_wait(barrier, n_experts - 1)
+
+    def hop(b, upward):
+        return pltpu.make_async_remote_copy(
+            src_ref=line.at[b], dst_ref=line.at[b],
+            send_sem=(up_sem if upward else down_sem).at[b], recv_sem=recv_sem.at[b],
+            device_id={"ep": lax.rem(me + 4, n) if upward else lax.rem(me + n - 4, n)},
+            device_id_type=MESH,
+        )
+
+    def swap(b):
+        return pltpu.make_async_remote_copy(
+            src_ref=x_out.at[b], dst_ref=x_in.at[b],
+            send_sem=x_send.at[b], recv_sem=x_recv.at[b],
+            device_id={"ep": partner}, device_id_type=MESH,
+        )
+
+    def back(b, other):
+        side = 1 - x if other else x
+        return pltpu.make_async_remote_copy(
+            src_ref=result.at[b, pl.ds(capacity * other, capacity)],
+            dst_ref=returned.at[pl.ds(pl.multiple_of(expert * capacity, capacity), capacity)],
+            send_sem=back_send.at[2 * b + other], recv_sem=back_recv.at[expert],
+            device_id={"ep": b * 4 + side * 2 + c}, device_id_type=MESH,
+        )
+
+    slots = lax.broadcasted_iota(jnp.int32, (capacity, rows), 0).astype(jnp.float32)
+    tile = 512
+    tiles = width // tile
+
+    def pack(b, e, put):
+        source = b * 4 + x * 2 + c
+        place = (codes_ref[source * n_experts + e] == slots).astype(jnp.bfloat16)
+
+        def step(i, carry):
+            col = pl.ds(pl.multiple_of(i * tile, tile), tile)
+            put(col, jnp.dot(
+                place, line[b, :, col], preferred_element_type=jnp.float32
+            ).astype(jnp.bfloat16))
+            return carry
+
+        lax.fori_loop(0, tiles, step, 0)
+
+    def arrive(b):
+        @pl.when(b != z)
+        def _():
+            hop(b, True).wait_recv()
+
+        @pl.when((b <= z) & (z < last))
+        def _():
+            hop(b, True).start()
+
+        @pl.when((b >= z) & (z > 0))
+        def _():
+            hop(b, False).start()
+
+        def put(col, value):
+            x_out[b, :, col] = value
+
+        pack(b, partner_expert, put)
+        swap(b).start()
+
+    def order(i):
+        low = jnp.minimum(z, last - z)
+        b = jnp.where((low == 1) & (i < 2), 1 - i, i)
+        return jnp.where(z < planes // 2, b, last - b)
+
+    def put_feed(col, value):
+        feed[0:capacity, col] = value
+
+    hidden_tile = 256
+
+    def step(i, carry):
+        b = order(i)
+        inner = (z > 0) & (z < last)
+
+        @pl.when((i != 2) | jnp.logical_not(inner))
+        def _():
+            arrive(b)
+
+        @pl.when((i == 1) & inner)
+        def _():
+            arrive(order(2))
+
+        pack(b, expert, put_feed)
+
+        @pl.when(i == 0)
+        def _():
+            for load in loads:
+                load.wait()
+
+        swap(b).wait_recv()
+        feed[capacity : 2 * capacity, :] = x_in[b]
+
+        def hidden_step(k, inner_carry):
+            col = pl.ds(pl.multiple_of(k * hidden_tile, hidden_tile), hidden_tile)
+            gate = jnp.dot(feed[...], w_gate[:, col], preferred_element_type=jnp.float32)
+            upward = jnp.dot(feed[...], w_up[:, col], preferred_element_type=jnp.float32)
+            hidden[:, col] = (jax.nn.silu(gate) * upward).astype(jnp.bfloat16)
+            return inner_carry
+
+        lax.fori_loop(0, 2 * ffe // hidden_tile, hidden_step, 0)
+
+        def down_step(k, inner_carry):
+            col = pl.ds(pl.multiple_of(k * tile, tile), tile)
+            result[b, :, col] = jnp.dot(
+                hidden[...], w_down[:, col], preferred_element_type=jnp.float32
+            ).astype(jnp.bfloat16)
+            return inner_carry
+
+        lax.fori_loop(0, tiles, down_step, 0)
+
+        back(b, 1).start()
+
+        @pl.when(b != z)
+        def _():
+            back(b, 0).start()
+
+        @pl.when(b == z)
+        def _():
+            returned[pl.ds(pl.multiple_of(expert * capacity, capacity), capacity), :] = result[
+                b, 0:capacity
+            ]
+
+        return carry
+
+    lax.fori_loop(0, planes, step, 0)
+
+    for e in range(n_experts):
+        @pl.when(expert != e)
+        def _():
+            pltpu.make_async_remote_copy(
+                src_ref=result.at[0, pl.ds(0, capacity)],
+                dst_ref=returned.at[pl.ds(e * capacity, capacity)],
+                send_sem=back_send.at[0], recv_sem=back_recv.at[e],
+                device_id={"ep": partner}, device_id_type=MESH,
+            ).wait_recv()
+
+    def mix_step(i, carry):
+        col = pl.ds(pl.multiple_of(i * tile, tile), tile)
+        picked = returned[:, col]
+        mixed = jnp.dot(hi_ref[...], picked, preferred_element_type=jnp.float32)
+        mixed += jnp.dot(lo_ref[...], picked, preferred_element_type=jnp.float32)
+        out_ref[:, col] = (stream_ref[:, col].astype(jnp.float32) + mixed).astype(jnp.bfloat16)
+        return carry
+
+    lax.fori_loop(0, tiles, mix_step, 0)
+
+    for b in range(planes):
+        @pl.when((b <= z) & (z < last))
+        def _():
+            hop(b, True).wait_send()
+
+        @pl.when((b >= z) & (z > 0))
+        def _():
+            hop(b, False).wait_send()
+
+        swap(b).wait_send()
+        back(b, 1).wait_send()
+
+        @pl.when(b != z)
+        def _():
+            back(b, 0).wait_send()
+
+
+def run_experts(n, capacity, tokens, stream, codes, mix_hi, mix_lo, weights):
+    rows, width = tokens.shape
+    ffe = weights[2].shape[0]
+    planes = n // 4
+    n_experts = n // 2
+    vmem = pl.BlockSpec(memory_space=pltpu.VMEM)
+    anywhere = pl.BlockSpec(memory_space=pl.ANY)
+    half = jnp.bfloat16
+    dma = pltpu.SemaphoreType.DMA
+    return pl.pallas_call(
+        functools.partial(experts_kernel, n, capacity),
+        out_shape=jax.ShapeDtypeStruct((rows, width), half),
+        in_specs=[vmem] * 5 + [anywhere] * 6,
+        out_specs=vmem,
+        scratch_shapes=[
+            pltpu.VMEM((planes, rows, width), half),
+            pltpu.VMEM((planes, capacity, width), half),
+            pltpu.VMEM((planes, capacity, width), half),
+            pltpu.VMEM((2 * capacity, width), half),
+            pltpu.VMEM((2 * capacity, 2 * ffe), half),
+            pltpu.VMEM((planes, 2 * capacity, width), half),
+            pltpu.VMEM((n_experts * capacity, width), half),
+            pltpu.VMEM((width, 2 * ffe), half),
+            pltpu.VMEM((width, 2 * ffe), half),
+            pltpu.VMEM((2 * ffe, width), half),
+            dma((6,)), dma((planes,)), dma((planes,)), dma((planes,)),
+            dma((planes,)), dma((planes,)), dma((2 * planes,)), dma((n_experts,)),
+        ],
+        compiler_params=pltpu.CompilerParams(
+            collective_id=1, has_side_effects=True, vmem_limit_bytes=56 * 1024 * 1024
+        ),
+        name="experts",
+    )(tokens, stream, codes, mix_hi, mix_lo, *weights)
 
 
 def local(
@@ -155,7 +402,6 @@
     capacity = max(2, 2 * rows * topk // n_experts)
 
     swap = [(i, i ^ 1) for i in range(n)]
-    core = lax.rem(lax.axis_index("ep"), 2)
     other_gate = lax.ppermute(w_gate[0], "ep", swap)
     other_up = lax.ppermute(w_up[0], "ep", swap)
     other_down = lax.ppermute(w_down[0], "ep", swap)
@@ -182,6 +428,12 @@
     mix_hi = mix.astype(jnp.bfloat16)
     mix_lo = (mix - mix_hi.astype(jnp.float32)).astype(jnp.bfloat16)
 
+    if n == 16:
+        codes = lax.all_gather(code.T.astype(jnp.float32), "ep").reshape(n * n_experts, 1, rows)
+        stream, normed = attention(n, kv_heads, queries, kv, segcol, residual, norm_gain[None, :])
+        weights = (w_gate[0], w_up[0], w_down[0], other_gate, other_up, other_down)
+        return run_experts(n, capacity, normed, stream, codes, mix_hi, mix_lo, weights)
+
     stream, outgoing = attention(n, kv_heads, queries, kv, segcol, residual, norm_gain[None, :], place)
 
     groups = [[c for c in range(k, n, 2)] for k in range(2)]

time: 308 us -> 267 us (0.87)
  waiting for transfers between devices: 187 us -> 0.01 us
  Pallas kernels: 53.6 us -> 219 us
  matrix products: 42.9 us -> 0.2 us
  blocking collectives: 0 us -> 28 us
  starting transfers between devices: 16.4 us -> 0.96 us
  local copies, waits for them, and re-layouts: 5.29 us -> 13.6 us
    all_to_all x2 -> x0, waiting for transfers between devices: 187 us -> none  [the longest x1 93.4 us: local(): lax.all_to_all(out.astype(jnp.bfloat16).reshape(n_experts, capacity, widt...]
    pallas_call x1 -> x2, Pallas kernels: 53.6 us -> 219 us  [the longest x1 168 us: run_experts(): pl.pallas_call(functools.partial(experts_kernel, n, capacity), out_shape=...]
    dot_general x6 -> x0, matrix products: 42.7 us -> none  [the longest x2 24.7 us: half(): return jnp.dot(hidden, down_half, preferred_element_type=jnp.float32)]
    all_gather x0 -> x1, blocking collectives: none -> 28 us  [local(): lax.all_gather(code.T.astype(jnp.float32), 'ep')]
    all_to_all x2 -> x0, starting transfers between devices: 15.4 us -> none  [the longest x1 10.7 us: local(): lax.all_to_all(outgoing.reshape(n_experts, capacity, width), 'ep', split_...]
    unnamed x10 -> x13, local copies, waits for them, and re-layouts: 4.38 us -> 8.33 us
  transfers between devices with their start and end apart: 5 -> 3, of which waited for: 2 -> 0; matrix products, arithmetic and copies ran while one was open for 7% -> 4% of each run, Pallas kernels for 0% -> 19%
where the time goes in v2:
time: 267 us
  Pallas kernels  219 us (82%)
  blocking collectives  28 us (10%)
  local copies, waits for them, and re-layouts  13.6 us (5%)
  other arithmetic  5.36 us (2%)
    pallas_call x1, Pallas kernels, run_experts(): pl.pallas_call(functools.partial(experts_kernel, n, capacity), out_shape=...  168 us
    pallas_call x1, Pallas kernels, attention(): pl.pallas_call(functools.partial(attention_kernel, n, kv_heads, placing),...  50.9 us
    all_gather x1, blocking collectives, local(): lax.all_gather(code.T.astype(jnp.float32), 'ep')  28 us
    unnamed x13, local copies, waits for them, and re-layouts  8.33 us
  transfers between devices with their start and end apart: 3, of which 0 were waited for; matrix products, arithmetic and copies ran while one was open for 4% of the time, Pallas kernels for 19%

profile of v2, /device:TPU:0, one launch (start us, length us, event | category | flops | bytes accessed | tf_op | source)
XLA Modules:
  0.0 267.0 jit_solution(16543132039351717050)
XLA Ops:
  0.0 0.5 collective-permute-start
  0.5 0.5 collective-permute-start.2
  1.0 0.7 broadcast_in_dim.55.gain_ref
  1.8 0.7 convert_bitcast_fusion.1
  2.5 0.1 copy.21.segcol_ref
  2.6 0.7 select_reduce_fusion
  3.3 0.7 broadcast_in_dim.61
  4.0 1.1 copy.23
  5.1 0.7 fusion.7
  5.8 0.2 fusion
  6.0 0.7 eq.36
  6.8 1.8 copy.22
  8.6 0.9 pad_maximum_fusion.kv_ref
  9.5 1.2 copy-done.2
  10.7 1.2 copy-done.3
  11.9 50.9 %attention.1 = (bf16[128,4096]{1,0:T(8,128)(2,1)S(1)}, bf16[128,4096]{1,0:T(8,128)(2,1)S(1)}) custom-call(bf16[128,4096]{1,0:T(8,128)(2,1)S(1)} %copy-done.2, bf16[144,512]{1,0:T(8,128)(2,1)S(1)} %pad_maximum_fusion.kv_ref, f32[128,1]{1,0:T(8,128)S(1)} %copy.21.segcol_ref, bf16[128,4096]{1,0:T(8,128)(2,1)S(1)} %copy-done.3, ...), custom_call_target="tpu_custom_call" | custom-call | tf_op jit(solution)/shard_map/attention/pallas_call | solution.py:137
  62.9 1.0 copy-done
  63.8 1.0 copy-done.1
  64.8 28.0 %all-gather = f32[128,128]{1,0:T(8,128)} all-gather(f32[8,128]{1,0:T(8,128)S(1)} %convert_bitcast_fusion), channel_id=2, replica_groups=mesh['group'=2,'ep'=16] {'ep'}, dimensions={0}, use_global_device_ids=true | all-gather | bytes 69632 | tf_op jit(solution)/shard_map/all_gather | solution.py:432
  92.8 1.6 subtract_convert_fusion.lo_ref
  94.5 0.7 fusion.1.hi_ref
  95.2 1.7 copy-done.4
  96.8 167.9 %experts.1 = bf16[128,4096]{1,0:T(8,128)(2,1)} custom-call(bf16[128,4096]{1,0:T(8,128)(2,1)} %copy-done.1, bf16[128,4096]{1,0:T(8,128)(2,1)} %copy-done, f32[128,1,128]{2,1,0:T(1,128)} %bitcast.19, bf16[128,512]{1,0:T(8,128)(2,1)} %fusion.1.hi_ref, bf16[128,512]{1,0:T(8,128)(2,1)} %subtract_convert_fusion.lo_ref, bf16[4096,384]{1,0:T(8,128)(2,1)} %bitcast.12, ...), custom_call_target="tpu_custom_call" | custom-call | tf_op jit(solution)/shard_map/experts/pallas_call | solution.py:367
  264.7 2.3 copy.25
  (17 shorter events, 0.2 us)
Async XLA Ops:
  0.0 95.1 %collective-permute-start = (bf16[4096,384]{1,0:T(8,128)(2,1)}, bf16[4096,384]{1,0:T(8,128)(2,1)S(1)}, u32[]{:S(2)}, u32[]{:S(2)}) collective-permute-start(bf16[4096,384]{1,0:T(8,128)(2,1)} %bitcast.11), channel_id=1, source_target_pairs={{0,1},{1,0},{2,3},{3,2},{4,5},{5,4},{6,7},{7,6},{8,9},{9,8},{10,11... | collective-permute-start | bytes 9437192 | tf_op jit(solution)/shard_map/ppermute | solution.py:405
  0.5 94.7 %collective-permute-start.1 = (bf16[4096,384]{1,0:T(8,128)(2,1)}, bf16[4096,384]{1,0:T(8,128)(2,1)}, u32[]{:S(2)}, u32[]{:S(2)}) collective-permute-start(bf16[4096,384]{1,0:T(8,128)(2,1)} %bitcast.13), channel_id=1, source_target_pairs={{0,1},{1,0},{2,3},{3,2},{4,5},{5,4},{6,7},{7,6},{8,9},{9,8},{10,11... | collective-permute-start | bytes 9437192 | tf_op jit(solution)/shard_map/ppermute | solution.py:406
  0.5 94.6 %collective-permute-start.2 = (bf16[384,4096]{1,0:T(8,128)(2,1)}, bf16[384,4096]{1,0:T(8,128)(2,1)}, u32[]{:S(2)}, u32[]{:S(2)}) collective-permute-start(bf16[384,4096]{1,0:T(8,128)(2,1)} %bitcast.15), channel_id=1, source_target_pairs={{0,1},{1,0},{2,3},{3,2},{4,5},{5,4},{6,7},{7,6},{8,9},{9,8},{10,11... | collective-permute-start | bytes 9437192 | tf_op jit(solution)/shard_map/ppermute | solution.py:407
  8.5 85.9 %copy-start.5 = (s32[128,512]{1,0:T(8,128)S(1)}, s32[128,512]{1,0:T(8,128)}, u32[]{:S(2)}) copy-start(s32[128,512]{1,0:T(8,128)} %copy.22) | copy-start | bytes 786436
  9.5 1.2 copy-start.2
  10.7 1.2 copy-start.3
  62.9 1.0 copy-start
  63.8 1.0 copy-start.1
  95.1 1.7 copy-start.4

commit v3 on v2

--- a/solution.py
+++ b/solution.py
@@ -23,15 +23,13 @@
     n, kv_heads, placing, q_ref, kv_ref, segcol_ref, res_ref, gain_ref, *rest
 ):
     if placing:
-        place_ref, stream_ref, rows_ref, held, bias, attended, normed, send_sem, recv_sem = rest
+        place_ref, stream_ref, rows_ref, held, bias, all_kv, attended, normed, send_sem, recv_sem = rest
     else:
-        stream_ref, normed, held, bias, attended, send_sem, recv_sem = rest
+        stream_ref, normed, held, bias, all_kv, attended, send_sem, recv_sem = rest
     me = lax.axis_index("ep")
     rows = q_ref.shape[0]
     heads = q_ref.shape[1] // HEAD_SIZE
     per_kv = heads // kv_heads
-    kv_width = kv_heads * HEAD_SIZE
-    span = rows + SEG_ROWS
     reach = min(REACH, n - 1)
 
     barrier = pltpu.get_barrier_semaphore()
@@ -61,35 +59,38 @@
         key_seg = held[d, rows : rows + SEG_ROWS, 0:rows][0:1].astype(jnp.float32)
         allowed = (key_seg == query_seg) & (u - d * rows <= t) & (u + (me - d) * rows >= 0)
         bias[:, d * rows : (d + 1) * rows] = jnp.where(allowed, 0.0, NEGATIVE)
+        for part in range(2 * kv_heads):
+            all_kv[part, d * rows : (d + 1) * rows, :] = held[
+                d, 0:rows, part * HEAD_SIZE : (part + 1) * HEAD_SIZE
+            ]
 
     scale = math.log2(math.e) / math.sqrt(HEAD_SIZE)
 
-    def one_head(h, g):
-        col = pl.multiple_of(h * HEAD_SIZE, HEAD_SIZE)
-        q = q_ref[:, pl.ds(col, HEAD_SIZE)]
-        k = jnp.concatenate(
-            [held[d, 0:rows, g * HEAD_SIZE : (g + 1) * HEAD_SIZE] for d in range(reach + 1)], 0
-        )
-        v = jnp.concatenate(
-            [
-                held[d, 0:rows, kv_width + g * HEAD_SIZE : kv_width + (g + 1) * HEAD_SIZE]
-                for d in range(reach + 1)
-            ],
-            0,
-        )
-        s = nt_dot(q, k) * scale + bias[...]
+    stack = 2
+
+    def some_heads(h, g):
+        cols = [
+            pl.ds(pl.multiple_of((h + j) * HEAD_SIZE, HEAD_SIZE), HEAD_SIZE) for j in range(stack)
+        ]
+        q = jnp.concatenate([q_ref[:, col] for col in cols], 0)
+        s = nt_dot(q, all_kv[g]) * scale
+        s = (s.reshape(stack, rows, s.shape[1]) + bias[...][None]).reshape(s.shape)
         top = jnp.max(s, -1, keepdims=True)
         p = jnp.exp2(s - top)
         total = jnp.sum(p, -1, keepdims=True)
-        pv = jnp.dot(p.astype(jnp.bfloat16), v, preferred_element_type=jnp.float32)
-        attended[:, pl.ds(col, HEAD_SIZE)] = (pv / total).astype(jnp.bfloat16)
+        pv = jnp.dot(
+            p.astype(jnp.bfloat16), all_kv[kv_heads + g], preferred_element_type=jnp.float32
+        )
+        done = (pv / total).astype(jnp.bfloat16)
+        for j, col in enumerate(cols):
+            attended[:, col] = done[j * rows : (j + 1) * rows]
 
     def heads_step(i, carry):
         for g in range(kv_heads):
-            one_head(i + g * per_kv, g)
+            some_heads(i * stack + g * per_kv, g)
         return carry
 
-    lax.fori_loop(0, per_kv, heads_step, 0)
+    lax.fori_loop(0, per_kv // stack, heads_step, 0)
 
     chunk = 16
 
@@ -130,6 +131,7 @@
     scratch = [
         pltpu.VMEM((reach + 1,) + kv.shape, jnp.bfloat16),
         pltpu.VMEM((rows, (reach + 1) * rows), jnp.float32),
+        pltpu.VMEM((2 * kv_heads, (reach + 1) * rows, HEAD_SIZE), jnp.bfloat16),
         pltpu.VMEM((rows, width), jnp.bfloat16),
     ]
     if placing:
@@ -157,8 +159,8 @@
     n, capacity, tokens_ref, stream_ref, codes_ref, hi_ref, lo_ref,
     gate0, up0, down0, gate1, up1, down1,
     out_ref,
-    line, x_out, x_in, feed, hidden, result, returned, w_gate, w_up, w_down,
-    w_sem, recv_sem, up_sem, down_sem, x_send, x_recv, back_send, back_recv,
+    line, codes, x_out, x_in, feed, hidden, result, returned, w_gate, w_up, w_down,
+    w_sem, recv_sem, up_sem, down_sem, code_recv, code_up, code_down, x_send, x_recv, back_send, back_recv,
 ):
     planes = n // 4
     n_experts = n // 2
@@ -190,14 +192,22 @@
             loads.append(load)
 
     line[z] = tokens_ref[...]
+    codes[z] = codes_ref[...]
     pl.semaphore_wait(barrier, n_experts - 1)
 
-    def hop(b, upward):
-        return pltpu.make_async_remote_copy(
-            src_ref=line.at[b], dst_ref=line.at[b],
-            send_sem=(up_sem if upward else down_sem).at[b], recv_sem=recv_sem.at[b],
-            device_id={"ep": lax.rem(me + 4, n) if upward else lax.rem(me + n - 4, n)},
-            device_id_type=MESH,
+    def hops(b, upward):
+        target = {"ep": lax.rem(me + 4, n) if upward else lax.rem(me + n - 4, n)}
+        return (
+            pltpu.make_async_remote_copy(
+                src_ref=codes.at[b], dst_ref=codes.at[b],
+                send_sem=(code_up if upward else code_down).at[b], recv_sem=code_recv.at[b],
+                device_id=target, device_id_type=MESH,
+            ),
+            pltpu.make_async_remote_copy(
+                src_ref=line.at[b], dst_ref=line.at[b],
+                send_sem=(up_sem if upward else down_sem).at[b], recv_sem=recv_sem.at[b],
+                device_id=target, device_id_type=MESH,
+            ),
         )
 
     def swap(b):
@@ -221,8 +231,7 @@
     tiles = width // tile
 
     def pack(b, e, put):
-        source = b * 4 + x * 2 + c
-        place = (codes_ref[source * n_experts + e] == slots).astype(jnp.bfloat16)
+        place = (codes[b, e] == slots).astype(jnp.bfloat16)
 
         def step(i, carry):
             col = pl.ds(pl.multiple_of(i * tile, tile), tile)
@@ -236,15 +245,18 @@
     def arrive(b):
         @pl.when(b != z)
         def _():
-            hop(b, True).wait_recv()
+            for copy in hops(b, True):
+                copy.wait_recv()
 
         @pl.when((b <= z) & (z < last))
         def _():
-            hop(b, True).start()
+            for copy in hops(b, True):
+                copy.start()
 
         @pl.when((b >= z) & (z > 0))
         def _():
-            hop(b, False).start()
+            for copy in hops(b, False):
+                copy.start()
 
         def put(col, value):
             x_out[b, :, col] = value
@@ -254,7 +266,7 @@
 
     def order(i):
         low = jnp.minimum(z, last - z)
-        b = jnp.where((low == 1) & (i < 2), 1 - i, i)
+        b = jnp.where((low == 1) & (i < 3), lax.rem(i + 1, 3), i)
         return jnp.where(z < planes // 2, b, last - b)
 
     def put_feed(col, value):
@@ -341,11 +353,13 @@
     for b in range(planes):
         @pl.when((b <= z) & (z < last))
         def _():
-            hop(b, True).wait_send()
+            for copy in hops(b, True):
+                copy.wait_send()
 
         @pl.when((b >= z) & (z > 0))
         def _():
-            hop(b, False).wait_send()
+            for copy in hops(b, False):
+                copy.wait_send()
 
         swap(b).wait_send()
         back(b, 1).wait_send()
@@ -371,6 +385,7 @@
         out_specs=vmem,
         scratch_shapes=[
             pltpu.VMEM((planes, rows, width), half),
+            pltpu.VMEM((planes, n_experts, 1, rows), jnp.float32),
             pltpu.VMEM((planes, capacity, width), half),
             pltpu.VMEM((planes, capacity, width), half),
             pltpu.VMEM((2 * capacity, width), half),
@@ -381,6 +396,7 @@
             pltpu.VMEM((width, 2 * ffe), half),
             pltpu.VMEM((2 * ffe, width), half),
             dma((6,)), dma((planes,)), dma((planes,)), dma((planes,)),
+            dma((planes,)), dma((planes,)), dma((planes,)),
             dma((planes,)), dma((planes,)), dma((2 * planes,)), dma((n_experts,)),
         ],
         compiler_params=pltpu.CompilerParams(
@@ -429,7 +445,7 @@
     mix_lo = (mix - mix_hi.astype(jnp.float32)).astype(jnp.bfloat16)
 
     if n == 16:
-        codes = lax.all_gather(code.T.astype(jnp.float32), "ep").reshape(n * n_experts, 1, rows)
+        codes = code.T.astype(jnp.float32).reshape(n_experts, 1, rows)
         stream, normed = attention(n, kv_heads, queries, kv, segcol, residual, norm_gain[None, :])
         weights = (w_gate[0], w_up[0], w_down[0], other_gate, other_up, other_down)
         return run_experts(n, capacity, normed, stream, codes, mix_hi, mix_lo, weights)

time: 267 us -> 273 us (1.022)
  Pallas kernels: 219 us -> 252 us
  blocking collectives: 28 us -> 0 us
    pallas_call x1, Pallas kernels: 168 us -> 206 us  [run_experts(): pl.pallas_call(functools.partial(experts_kernel, n, capacity), out_shape=...]
    all_gather x1 -> x0, blocking collectives: 28 us -> none  [local(): lax.all_gather(code.T.astype(jnp.float32), 'ep')]
    pallas_call x1, Pallas kernels: 50.9 us -> 46.5 us  [attention(): pl.pallas_call(functools.partial(attention_kernel, n, kv_heads, placing),...]
  transfers between devices with their start and end apart: 3 -> 3, of which waited for: 0 -> 0; matrix products, arithmetic and copies ran while one was open for 4% -> 4% of each run, Pallas kernels for 19% -> 17%
where the time goes in v3:
time: 273 us
  Pallas kernels  252 us (92%)
  local copies, waits for them, and re-layouts  13.6 us (5%)
  other arithmetic  5.39 us (2%)
    pallas_call x1, Pallas kernels, run_experts(): pl.pallas_call(functools.partial(experts_kernel, n, capacity), out_shape=...  206 us
    pallas_call x1, Pallas kernels, attention(): pl.pallas_call(functools.partial(attention_kernel, n, kv_heads, placing),...  46.5 us
    unnamed x13, local copies, waits for them, and re-layouts  8.35 us
  transfers between devices with their start and end apart: 3, of which 0 were waited for; matrix products, arithmetic and copies ran while one was open for 4% of the time, Pallas kernels for 17%

profile of v3, /device:TPU:0, one launch (start us, length us, event | category | flops | bytes accessed | tf_op | source)
XLA Modules:
  0.0 272.9 jit_solution(10472254472641882567)
XLA Ops:
  0.0 0.5 collective-permute-start
  0.5 0.5 collective-permute-start.2
  1.0 0.1 eq.39
  1.0 0.7 broadcast_in_dim.55.gain_ref
  1.8 0.7 convert_bitcast_fusion
  2.5 0.1 copy.21.segcol_ref
  2.6 0.7 select_reduce_fusion
  3.3 0.7 broadcast_in_dim.61
  4.0 1.1 copy.23
  5.1 0.7 fusion.7
  5.8 0.8 fusion.10
  6.6 0.7 eq.36
  7.3 1.8 copy.22
  9.1 0.9 pad_maximum_fusion.kv_ref
  10.1 1.2 copy-done.2
  11.3 1.2 copy-done.3
  12.5 46.5 %attention.1 = (bf16[128,4096]{1,0:T(8,128)(2,1)S(1)}, bf16[128,4096]{1,0:T(8,128)(2,1)S(1)}) custom-call(bf16[128,4096]{1,0:T(8,128)(2,1)S(1)} %copy-done.2, bf16[144,512]{1,0:T(8,128)(2,1)S(1)} %pad_maximum_fusion.kv_ref, f32[128,1]{1,0:T(8,128)S(1)} %copy.21.segcol_ref, bf16[128,4096]{1,0:T(8,128)(2,1)S(1)} %copy-done.3, ...), custom_call_target="tpu_custom_call" | custom-call | tf_op jit(solution)/shard_map/attention/pallas_call | solution.py:139
  59.0 1.0 copy-done
  60.0 1.0 copy-done.1
  60.9 1.6 subtract_convert_fusion.lo_ref
  62.6 0.7 fusion.1.hi_ref
  63.3 1.7 copy-done.4
  65.0 205.6 %experts.1 = bf16[128,4096]{1,0:T(8,128)(2,1)} custom-call(bf16[128,4096]{1,0:T(8,128)(2,1)} %copy-done.1, bf16[128,4096]{1,0:T(8,128)(2,1)} %copy-done, f32[8,1,128]{2,1,0:T(1,128)} %bitcast.19, bf16[128,512]{1,0:T(8,128)(2,1)} %fusion.1.hi_ref, bf16[128,512]{1,0:T(8,128)(2,1)} %subtract_convert_fusion.lo_ref, bf16[4096,384]{1,0:T(8,128)(2,1)} %bitcast.12, ...), custom_call_target="tpu_custom_call" | custom-call | tf_op jit(solution)/shard_map/experts/pallas_call | solution.py:381
  270.6 2.3 copy.25
  (15 shorter events, 0.1 us)
Async XLA Ops:
  0.0 63.3 %collective-permute-start = (bf16[4096,384]{1,0:T(8,128)(2,1)}, bf16[4096,384]{1,0:T(8,128)(2,1)S(1)}, u32[]{:S(2)}, u32[]{:S(2)}) collective-permute-start(bf16[4096,384]{1,0:T(8,128)(2,1)} %bitcast.11), channel_id=1, source_target_pairs={{0,1},{1,0},{2,3},{3,2},{4,5},{5,4},{6,7},{7,6},{8,9},{9,8},{10,11... | collective-permute-start | bytes 9437192 | tf_op jit(solution)/shard_map/ppermute | solution.py:421
  0.5 62.8 %collective-permute-start.1 = (bf16[4096,384]{1,0:T(8,128)(2,1)}, bf16[4096,384]{1,0:T(8,128)(2,1)}, u32[]{:S(2)}, u32[]{:S(2)}) collective-permute-start(bf16[4096,384]{1,0:T(8,128)(2,1)} %bitcast.13), channel_id=1, source_target_pairs={{0,1},{1,0},{2,3},{3,2},{4,5},{5,4},{6,7},{7,6},{8,9},{9,8},{10,11... | collective-permute-start | bytes 9437192 | tf_op jit(solution)/shard_map/ppermute | solution.py:422
  0.5 62.8 %collective-permute-start.2 = (bf16[384,4096]{1,0:T(8,128)(2,1)}, bf16[384,4096]{1,0:T(8,128)(2,1)}, u32[]{:S(2)}, u32[]{:S(2)}) collective-permute-start(bf16[384,4096]{1,0:T(8,128)(2,1)} %bitcast.15), channel_id=1, source_target_pairs={{0,1},{1,0},{2,3},{3,2},{4,5},{5,4},{6,7},{7,6},{8,9},{9,8},{10,11... | collective-permute-start | bytes 9437192 | tf_op jit(solution)/shard_map/ppermute | solution.py:423
  9.1 53.5 %copy-start.5 = (s32[128,512]{1,0:T(8,128)S(1)}, s32[128,512]{1,0:T(8,128)}, u32[]{:S(2)}) copy-start(s32[128,512]{1,0:T(8,128)} %copy.22) | copy-start | bytes 786436
  10.1 1.2 copy-start.2
  11.3 1.2 copy-start.3
  59.0 1.0 copy-start
  60.0 1.0 copy-start.1
  63.3 1.7 copy-start.4

commit v4 on v3

--- a/solution.py
+++ b/solution.py
@@ -266,7 +266,7 @@
 
     def order(i):
         low = jnp.minimum(z, last - z)
-        b = jnp.where((low == 1) & (i < 3), lax.rem(i + 1, 3), i)
+        b = jnp.where((low == 1) & (i < 2), 1 - i, i)
         return jnp.where(z < planes // 2, b, last - b)
 
     def put_feed(col, value):

time: 273 us -> 244 us (0.89)
  Pallas kernels: 252 us -> 223 us
    pallas_call x1, Pallas kernels: 206 us -> 177 us  [run_experts(): pl.pallas_call(functools.partial(experts_kernel, n, capacity), out_shape=...]
  transfers between devices with their start and end apart: 3 -> 3, of which waited for: 0 -> 0; matrix products, arithmetic and copies ran while one was open for 4% -> 5% of each run, Pallas kernels for 17% -> 19%
where the time goes in v4:
time: 244 us
  Pallas kernels  223 us (91%)
  local copies, waits for them, and re-layouts  13.6 us (6%)
  other arithmetic  5.39 us (2%)
    pallas_call x1, Pallas kernels, run_experts(): pl.pallas_call(functools.partial(experts_kernel, n, capacity), out_shape=...  177 us
    pallas_call x1, Pallas kernels, attention(): pl.pallas_call(functools.partial(attention_kernel, n, kv_heads, placing),...  46.5 us
    unnamed x13, local copies, waits for them, and re-layouts  8.35 us
  transfers between devices with their start and end apart: 3, of which 0 were waited for; matrix products, arithmetic and copies ran while one was open for 5% of the time, Pallas kernels for 19%

profile of v4, /device:TPU:0, one launch (start us, length us, event | category | flops | bytes accessed | tf_op | source)
XLA Modules:
  0.0 243.8 jit_solution(1740053566583848734)
XLA Ops:
  0.0 0.5 collective-permute-start
  0.5 0.5 collective-permute-start.2
  1.0 0.1 eq.39
  1.0 0.7 broadcast_in_dim.55.gain_ref
  1.8 0.7 convert_bitcast_fusion
  2.5 0.1 copy.21.segcol_ref
  2.6 0.7 select_reduce_fusion
  3.3 0.7 broadcast_in_dim.61
  4.0 1.1 copy.23
  5.1 0.7 fusion.7
  5.8 0.8 fusion.10
  6.6 0.7 eq.36
  7.3 1.8 copy.22
  9.1 0.9 pad_maximum_fusion.kv_ref
  10.1 1.2 copy-done.2
  11.3 1.2 copy-done.3
  12.5 46.5 %attention.1 = (bf16[128,4096]{1,0:T(8,128)(2,1)S(1)}, bf16[128,4096]{1,0:T(8,128)(2,1)S(1)}) custom-call(bf16[128,4096]{1,0:T(8,128)(2,1)S(1)} %copy-done.2, bf16[144,512]{1,0:T(8,128)(2,1)S(1)} %pad_maximum_fusion.kv_ref, f32[128,1]{1,0:T(8,128)S(1)} %copy.21.segcol_ref, bf16[128,4096]{1,0:T(8,128)(2,1)S(1)} %copy-done.3, ...), custom_call_target="tpu_custom_call" | custom-call | tf_op jit(solution)/shard_map/attention/pallas_call | solution.py:139
  59.0 1.0 copy-done
  60.0 1.0 copy-done.1
  60.9 1.6 subtract_convert_fusion.lo_ref
  62.6 0.7 fusion.1.hi_ref
  63.3 1.7 copy-done.4
  65.0 176.5 %experts.1 = bf16[128,4096]{1,0:T(8,128)(2,1)} custom-call(bf16[128,4096]{1,0:T(8,128)(2,1)} %copy-done.1, bf16[128,4096]{1,0:T(8,128)(2,1)} %copy-done, f32[8,1,128]{2,1,0:T(1,128)} %bitcast.19, bf16[128,512]{1,0:T(8,128)(2,1)} %fusion.1.hi_ref, bf16[128,512]{1,0:T(8,128)(2,1)} %subtract_convert_fusion.lo_ref, bf16[4096,384]{1,0:T(8,128)(2,1)} %bitcast.12, ...), custom_call_target="tpu_custom_call" | custom-call | tf_op jit(solution)/shard_map/experts/pallas_call | solution.py:381
  241.5 2.3 copy.25
  (15 shorter events, 0.1 us)
Async XLA Ops:
  0.0 63.3 %collective-permute-start = (bf16[4096,384]{1,0:T(8,128)(2,1)}, bf16[4096,384]{1,0:T(8,128)(2,1)S(1)}, u32[]{:S(2)}, u32[]{:S(2)}) collective-permute-start(bf16[4096,384]{1,0:T(8,128)(2,1)} %bitcast.11), channel_id=1, source_target_pairs={{0,1},{1,0},{2,3},{3,2},{4,5},{5,4},{6,7},{7,6},{8,9},{9,8},{10,11... | collective-permute-start | bytes 9437192 | tf_op jit(solution)/shard_map/ppermute | solution.py:421
  0.5 62.8 %collective-permute-start.1 = (bf16[4096,384]{1,0:T(8,128)(2,1)}, bf16[4096,384]{1,0:T(8,128)(2,1)}, u32[]{:S(2)}, u32[]{:S(2)}) collective-permute-start(bf16[4096,384]{1,0:T(8,128)(2,1)} %bitcast.13), channel_id=1, source_target_pairs={{0,1},{1,0},{2,3},{3,2},{4,5},{5,4},{6,7},{7,6},{8,9},{9,8},{10,11... | collective-permute-start | bytes 9437192 | tf_op jit(solution)/shard_map/ppermute | solution.py:422
  0.5 62.8 %collective-permute-start.2 = (bf16[384,4096]{1,0:T(8,128)(2,1)}, bf16[384,4096]{1,0:T(8,128)(2,1)}, u32[]{:S(2)}, u32[]{:S(2)}) collective-permute-start(bf16[384,4096]{1,0:T(8,128)(2,1)} %bitcast.15), channel_id=1, source_target_pairs={{0,1},{1,0},{2,3},{3,2},{4,5},{5,4},{6,7},{7,6},{8,9},{9,8},{10,11... | collective-permute-start | bytes 9437192 | tf_op jit(solution)/shard_map/ppermute | solution.py:423
  9.1 53.5 %copy-start.5 = (s32[128,512]{1,0:T(8,128)S(1)}, s32[128,512]{1,0:T(8,128)}, u32[]{:S(2)}) copy-start(s32[128,512]{1,0:T(8,128)} %copy.22) | copy-start | bytes 786436
  10.1 1.2 copy-start.2
  11.3 1.2 copy-start.3
  59.0 1.0 copy-start
  60.0 1.0 copy-start.1
  63.3 1.7 copy-start.4

commit v5 on v4

--- a/solution.py
+++ b/solution.py
@@ -30,27 +30,54 @@
     rows = q_ref.shape[0]
     heads = q_ref.shape[1] // HEAD_SIZE
     per_kv = heads // kv_heads
-    reach = min(REACH, n - 1)
+    reach = min(REACH, n - 2)
+
+    core = lax.rem(me, 2)
+    sibling = me + 1 - 2 * core
+    steps = range(2, reach + 1, 2)
 
     barrier = pltpu.get_barrier_semaphore()
-    for d in range(1, reach + 1):
+    for d in steps:
         pl.semaphore_signal(
             barrier, inc=1, device_id={"ep": lax.rem(me + n - d, n)}, device_id_type=MESH
         )
-    pl.semaphore_wait(barrier, reach)
-
-    copies = []
-    for d in range(1, reach + 1):
-        copy = pltpu.make_async_remote_copy(
+    pl.semaphore_signal(barrier, inc=1, device_id={"ep": sibling}, device_id_type=MESH)
+    pl.semaphore_wait(barrier, len(steps) + 1)
+
+    def direct(d):
+        return pltpu.make_async_remote_copy(
             src_ref=kv_ref, dst_ref=held.at[d],
             send_sem=send_sem.at[d], recv_sem=recv_sem.at[d],
             device_id={"ep": lax.rem(me + d, n)}, device_id_type=MESH,
         )
-        copy.start()
-        copies.append(copy)
+
+    def passed_on(k):
+        return pltpu.make_async_remote_copy(
+            src_ref=held.at[2 * k + 2 * core], dst_ref=held.at[2 * k + 1],
+            send_sem=send_sem.at[2 * k + 1], recv_sem=recv_sem.at[2 * k + 1],
+            device_id={"ep": sibling}, device_id_type=MESH,
+        )
+
+    for d in steps:
+        direct(d).start()
     held[0] = kv_ref[...]
-    for copy in copies:
-        copy.wait()
+    for k in range(reach // 2):
+        if k == 0:
+            @pl.when(core == 1)
+            def _():
+                direct(2).wait_recv()
+        else:
+            direct(2 * k + 2 * core).wait_recv()
+        passed_on(k).start()
+
+    @pl.when(core == 0)
+    def _():
+        direct(reach).wait_recv()
+
+    for k in range(reach // 2):
+        passed_on(k).wait()
+    for d in steps:
+        direct(d).wait_send()
 
     query_seg = segcol_ref[...]
     t = lax.broadcasted_iota(jnp.int32, (rows, rows), 0)
@@ -123,7 +150,7 @@
 
 def attention(n, kv_heads, queries, kv, segcol, residual, gain, place=None):
     rows, width = queries.shape
-    reach = min(REACH, n - 1)
+    reach = min(REACH, n - 2)
     vmem = pl.BlockSpec(memory_space=pltpu.VMEM)
     placing = place is not None
     sent = place.shape[0] if placing else rows

time: 244 us -> 228 us (0.934)
  Pallas kernels: 223 us -> 207 us
    pallas_call x1, Pallas kernels: 46.5 us -> 36.5 us  [attention(): pl.pallas_call(functools.partial(attention_kernel, n, kv_heads, placing),...]
    pallas_call x1, Pallas kernels: 177 us -> 170 us  [run_experts(): pl.pallas_call(functools.partial(experts_kernel, n, capacity), out_shape=...]
  transfers between devices with their start and end apart: 3 -> 3, of which waited for: 0 -> 0; matrix products, arithmetic and copies ran while one was open for 5% -> 5% of each run, Pallas kernels for 19% -> 16%
where the time goes in v5:
time: 228 us
  Pallas kernels  207 us (91%)
  local copies, waits for them, and re-layouts  13.6 us (6%)
  other arithmetic  5.39 us (2%)
    pallas_call x1, Pallas kernels, run_experts(): pl.pallas_call(functools.partial(experts_kernel, n, capacity), out_shape=...  170 us
    pallas_call x1, Pallas kernels, attention(): pl.pallas_call(functools.partial(attention_kernel, n, kv_heads, placing),...  36.5 us
    unnamed x13, local copies, waits for them, and re-layouts  8.35 us
  transfers between devices with their start and end apart: 3, of which 0 were waited for; matrix products, arithmetic and copies ran while one was open for 5% of the time, Pallas kernels for 16%

profile of v5, /device:TPU:0, one launch (start us, length us, event | category | flops | bytes accessed | tf_op | source)
XLA Modules:
  0.0 227.5 jit_solution(18154912761227682512)
XLA Ops:
  0.0 0.5 collective-permute-start
  0.5 0.5 collective-permute-start.2
  1.0 0.1 eq.39
  1.0 0.7 broadcast_in_dim.55.gain_ref
  1.8 0.7 convert_bitcast_fusion
  2.5 0.1 copy.21.segcol_ref
  2.6 0.7 select_reduce_fusion
  3.3 0.7 broadcast_in_dim.61
  4.0 1.1 copy.23
  5.1 0.7 fusion.7
  5.8 0.8 fusion.10
  6.6 0.7 eq.36
  7.3 1.8 copy.22
  9.1 0.9 pad_maximum_fusion.kv_ref
  10.1 1.2 copy-done.2
  11.3 1.2 copy-done.3
  12.5 36.5 %attention.1 = (bf16[128,4096]{1,0:T(8,128)(2,1)S(1)}, bf16[128,4096]{1,0:T(8,128)(2,1)S(1)}) custom-call(bf16[128,4096]{1,0:T(8,128)(2,1)S(1)} %copy-done.2, bf16[144,512]{1,0:T(8,128)(2,1)S(1)} %pad_maximum_fusion.kv_ref, f32[128,1]{1,0:T(8,128)S(1)} %copy.21.segcol_ref, bf16[128,4096]{1,0:T(8,128)(2,1)S(1)} %copy-done.3, ...), custom_call_target="tpu_custom_call" | custom-call | tf_op jit(solution)/shard_map/attention/pallas_call | solution.py:166
  49.0 1.0 copy-done
  50.0 1.0 copy-done.1
  51.0 1.6 subtract_convert_fusion.lo_ref
  52.6 0.7 fusion.1.hi_ref
  53.3 1.7 copy-done.4
  55.0 170.2 %experts.1 = bf16[128,4096]{1,0:T(8,128)(2,1)} custom-call(bf16[128,4096]{1,0:T(8,128)(2,1)} %copy-done.1, bf16[128,4096]{1,0:T(8,128)(2,1)} %copy-done, f32[8,1,128]{2,1,0:T(1,128)} %bitcast.19, bf16[128,512]{1,0:T(8,128)(2,1)} %fusion.1.hi_ref, bf16[128,512]{1,0:T(8,128)(2,1)} %subtract_convert_fusion.lo_ref, bf16[4096,384]{1,0:T(8,128)(2,1)} %bitcast.12, ...), custom_call_target="tpu_custom_call" | custom-call | tf_op jit(solution)/shard_map/experts/pallas_call | solution.py:408
  225.3 2.3 %copy.25 = bf16[128,4096]{1,0:T(8,128)(2,1)} copy(bf16[128,4096]{1,0:T(8,128)(2,1)} %experts.1) | data formatting | bytes 2097152
  (15 shorter events, 0.1 us)
Async XLA Ops:
  0.0 53.3 %collective-permute-start = (bf16[4096,384]{1,0:T(8,128)(2,1)}, bf16[4096,384]{1,0:T(8,128)(2,1)S(1)}, u32[]{:S(2)}, u32[]{:S(2)}) collective-permute-start(bf16[4096,384]{1,0:T(8,128)(2,1)} %bitcast.11), channel_id=1, source_target_pairs={{0,1},{1,0},{2,3},{3,2},{4,5},{5,4},{6,7},{7,6},{8,9},{9,8},{10,11... | collective-permute-start | bytes 9437192 | tf_op jit(solution)/shard_map/ppermute | solution.py:448
  0.5 52.9 %collective-permute-start.1 = (bf16[4096,384]{1,0:T(8,128)(2,1)}, bf16[4096,384]{1,0:T(8,128)(2,1)}, u32[]{:S(2)}, u32[]{:S(2)}) collective-permute-start(bf16[4096,384]{1,0:T(8,128)(2,1)} %bitcast.13), channel_id=1, source_target_pairs={{0,1},{1,0},{2,3},{3,2},{4,5},{5,4},{6,7},{7,6},{8,9},{9,8},{10,11... | collective-permute-start | bytes 9437192 | tf_op jit(solution)/shard_map/ppermute | solution.py:449
  0.5 52.8 %collective-permute-start.2 = (bf16[384,4096]{1,0:T(8,128)(2,1)}, bf16[384,4096]{1,0:T(8,128)(2,1)}, u32[]{:S(2)}, u32[]{:S(2)}) collective-permute-start(bf16[384,4096]{1,0:T(8,128)(2,1)} %bitcast.15), channel_id=1, source_target_pairs={{0,1},{1,0},{2,3},{3,2},{4,5},{5,4},{6,7},{7,6},{8,9},{9,8},{10,11... | collective-permute-start | bytes 9437192 | tf_op jit(solution)/shard_map/ppermute | solution.py:450
  9.1 43.5 %copy-start.5 = (s32[128,512]{1,0:T(8,128)S(1)}, s32[128,512]{1,0:T(8,128)}, u32[]{:S(2)}) copy-start(s32[128,512]{1,0:T(8,128)} %copy.22) | copy-start | bytes 786436
  10.1 1.2 copy-start.2
  11.3 1.2 copy-start.3
  49.0 1.0 copy-start
  50.0 1.0 copy-start.1
  53.3 1.7 copy-start.4

commit v6 on v5

--- a/solution.py
+++ b/solution.py
@@ -93,7 +93,7 @@
 
     scale = math.log2(math.e) / math.sqrt(HEAD_SIZE)
 
-    stack = 2
+    stack = 4
 
     def some_heads(h, g):
         cols = [

time: 228 us -> 228 us (level)
  no operation moved by 1% of the time
where the time goes in v6:
time: 228 us; the launch traced here: 227 us
  Pallas kernels  206 us (90%)
  local copies, waits for them, and re-layouts  13.6 us (6%)
  other arithmetic  5.39 us (2%)
    pallas_call x1, Pallas kernels, run_experts(): pl.pallas_call(functools.partial(experts_kernel, n, capacity), out_shape=...  170 us
    pallas_call x1, Pallas kernels, attention(): pl.pallas_call(functools.partial(attention_kernel, n, kv_heads, placing),...  36.2 us
    unnamed x13, local copies, waits for them, and re-layouts  8.35 us
  transfers between devices with their start and end apart: 3, of which 0 were waited for; matrix products, arithmetic and copies ran while one was open for 5% of the time, Pallas kernels for 16%

profile of v6, /device:TPU:0, one launch (start us, length us, event | category | flops | bytes accessed | tf_op | source)
XLA Modules:
  0.0 227.2 jit_solution(16182887484210676589)
XLA Ops:
  0.0 0.5 collective-permute-start
  0.5 0.5 collective-permute-start.2
  1.0 0.1 eq.39
  1.0 0.7 broadcast_in_dim.55.gain_ref
  1.8 0.7 convert_bitcast_fusion
  2.5 0.1 copy.21.segcol_ref
  2.6 0.7 select_reduce_fusion
  3.3 0.7 broadcast_in_dim.61
  4.0 1.1 copy.23
  5.1 0.7 fusion.7
  5.8 0.8 fusion.10
  6.6 0.7 eq.36
  7.3 1.8 copy.22
  9.1 0.9 pad_maximum_fusion.kv_ref
  10.1 1.2 copy-done.2
  11.3 1.2 copy-done.3
  12.5 36.2 %attention.1 = (bf16[128,4096]{1,0:T(8,128)(2,1)S(1)}, bf16[128,4096]{1,0:T(8,128)(2,1)S(1)}) custom-call(bf16[128,4096]{1,0:T(8,128)(2,1)S(1)} %copy-done.2, bf16[144,512]{1,0:T(8,128)(2,1)S(1)} %pad_maximum_fusion.kv_ref, f32[128,1]{1,0:T(8,128)S(1)} %copy.21.segcol_ref, bf16[128,4096]{1,0:T(8,128)(2,1)S(1)} %copy-done.3, ...), custom_call_target="tpu_custom_call" | custom-call | tf_op jit(solution)/shard_map/attention/pallas_call | solution.py:166
  48.7 1.0 copy-done
  49.6 1.0 copy-done.1
  50.6 1.6 subtract_convert_fusion.lo_ref
  52.3 0.7 fusion.1.hi_ref
  53.0 1.7 copy-done.4
  54.7 170.2 %experts.1 = bf16[128,4096]{1,0:T(8,128)(2,1)} custom-call(bf16[128,4096]{1,0:T(8,128)(2,1)} %copy-done.1, bf16[128,4096]{1,0:T(8,128)(2,1)} %copy-done, f32[8,1,128]{2,1,0:T(1,128)} %bitcast.19, bf16[128,512]{1,0:T(8,128)(2,1)} %fusion.1.hi_ref, bf16[128,512]{1,0:T(8,128)(2,1)} %subtract_convert_fusion.lo_ref, bf16[4096,384]{1,0:T(8,128)(2,1)} %bitcast.12, ...), custom_call_target="tpu_custom_call" | custom-call | tf_op jit(solution)/shard_map/experts/pallas_call | solution.py:408
  224.9 2.3 %copy.25 = bf16[128,4096]{1,0:T(8,128)(2,1)} copy(bf16[128,4096]{1,0:T(8,128)(2,1)} %experts.1) | data formatting | bytes 2097152
  (15 shorter events, 0.1 us)
Async XLA Ops:
  0.0 53.0 %collective-permute-start = (bf16[4096,384]{1,0:T(8,128)(2,1)}, bf16[4096,384]{1,0:T(8,128)(2,1)S(1)}, u32[]{:S(2)}, u32[]{:S(2)}) collective-permute-start(bf16[4096,384]{1,0:T(8,128)(2,1)} %bitcast.11), channel_id=1, source_target_pairs={{0,1},{1,0},{2,3},{3,2},{4,5},{5,4},{6,7},{7,6},{8,9},{9,8},{10,11... | collective-permute-start | bytes 9437192 | tf_op jit(solution)/shard_map/ppermute | solution.py:448
  0.5 52.5 %collective-permute-start.1 = (bf16[4096,384]{1,0:T(8,128)(2,1)}, bf16[4096,384]{1,0:T(8,128)(2,1)}, u32[]{:S(2)}, u32[]{:S(2)}) collective-permute-start(bf16[4096,384]{1,0:T(8,128)(2,1)} %bitcast.13), channel_id=1, source_target_pairs={{0,1},{1,0},{2,3},{3,2},{4,5},{5,4},{6,7},{7,6},{8,9},{9,8},{10,11... | collective-permute-start | bytes 9437192 | tf_op jit(solution)/shard_map/ppermute | solution.py:449
  0.5 52.5 %collective-permute-start.2 = (bf16[384,4096]{1,0:T(8,128)(2,1)}, bf16[384,4096]{1,0:T(8,128)(2,1)}, u32[]{:S(2)}, u32[]{:S(2)}) collective-permute-start(bf16[384,4096]{1,0:T(8,128)(2,1)} %bitcast.15), channel_id=1, source_target_pairs={{0,1},{1,0},{2,3},{3,2},{4,5},{5,4},{6,7},{7,6},{8,9},{9,8},{10,11... | collective-permute-start | bytes 9437192 | tf_op jit(solution)/shard_map/ppermute | solution.py:450
  9.1 43.1 %copy-start.5 = (s32[128,512]{1,0:T(8,128)S(1)}, s32[128,512]{1,0:T(8,128)}, u32[]{:S(2)}) copy-start(s32[128,512]{1,0:T(8,128)} %copy.22) | copy-start | bytes 786436
  10.1 1.2 copy-start.2
  11.3 1.2 copy-start.3
  48.7 1.0 copy-start
  49.6 1.0 copy-start.1
  53.0 1.7 copy-start.4
